TPU v7x, 128 devices: a whole 4x4x4 slice. The times are simulated.
128 devices in a mesh: dp: 2 (over z_lo), fsdp: 8 (over x, core), seq: 8 (over z_hi, y).
Axes of the slice: x: 4, y: 4, z: 4 (z_hi: 2, z_lo: 2; z = z_hi * 2 + z_lo), core: 2. Of those that a mesh axis runs over, the one named last changes fastest.
Arguments:
- tokens: bfloat16 [2, 32, 8, 8, 4096], P('dp', 'seq', None, None, 'fsdp'), may hold values from -6 to 6
- grad_out: bfloat16 [2, 32, 8, 8, 4096], P('dp', 'seq', None, None, 'fsdp'), may hold values from -6 to 6
- gain: float32 [4096], P('fsdp'), may hold values from 0.1 to 1.9
- up_weight: bfloat16 [4096, 8192], P('seq', 'fsdp'), may hold values from -0.09375 to 0.09375
- down_weight: bfloat16 [8192, 4096], P('fsdp', 'seq'), may hold values from -0.0625 to 0.0625
- conv_taps: float32 [27, 8192], P(None, 'fsdp'), may hold values from -1.25 to 1.25
Outputs:
- mixed: bfloat16 [2, 32, 8, 8, 4096], P('dp', 'seq', None, None, 'fsdp')
- grad_tokens: bfloat16 [2, 32, 8, 8, 4096], P('dp', 'seq', None, None, 'fsdp')
- grad_up: bfloat16 [4096, 8192], P('seq', 'fsdp')
- grad_down: bfloat16 [8192, 4096], P('fsdp', 'seq')
- grad_conv: float32 [27, 8192], P(None, 'fsdp')
- grad_gain: float32 [4096], P('fsdp')
All inputs are finite; a program needn't handle non-finite values.
Results may differ from a plain program's by a relative error of at most 0.025.
Values may be sent and summed in bfloat16 or wider, within the bound.
A program may use at most 128 MiB of HBM per device.

v0:
```python
import jax
import jax.numpy as jnp
from jax import lax
from jax.sharding import PartitionSpec as P

gelu_scale = 0.7978845608028654
gelu_cubic = 0.044715
epsilon = 1e-06


def with_halo(block, sides, width):
    for axis, dim in sides:
        count = lax.axis_size(axis)
        forward = [(i, i + 1) for i in range(count - 1)]
        backward = [(target, source) for source, target in forward]
        low = lax.ppermute(
            lax.slice_in_dim(block, block.shape[dim] - width, None, axis=dim), axis, forward
        )
        high = lax.ppermute(lax.slice_in_dim(block, 0, width, axis=dim), axis, backward)
        block = jnp.concatenate([low, block, high], axis=dim)
    return block


def gelu_pair(preact):
    inner = gelu_scale * (preact + gelu_cubic * preact * preact * preact)
    tangent = jnp.tanh(inner)
    value = 0.5 * preact * (1.0 + tangent)
    slope = 0.5 * (1.0 + tangent) + 0.5 * preact * (1.0 - tangent * tangent) * gelu_scale * (
        1.0 + 3.0 * gelu_cubic * preact * preact
    )
    return (value, slope)


def pad_sides(field):
    return jnp.pad(field, ((0, 0), (0, 0), (1, 1), (1, 1), (0, 0)))


def conv_apply(padded, kernel, flipped):
    planes = padded.shape[1] - 2
    side_y = padded.shape[2] - 2
    side_z = padded.shape[3] - 2
    total = jnp.zeros((padded.shape[0], planes, side_y, side_z, padded.shape[4]), jnp.float32)
    for shift_x in range(3):
        for shift_y in range(3):
            for shift_z in range(3):
                tap_row = kernel[shift_x * 9 + shift_y * 3 + shift_z]
                if flipped:
                    begin_x, begin_y, begin_z = (2 - shift_x, 2 - shift_y, 2 - shift_z)
                else:
                    begin_x, begin_y, begin_z = (shift_x, shift_y, shift_z)
                window = padded[
                    :,
                    begin_x : begin_x + planes,
                    begin_y : begin_y + side_y,
                    begin_z : begin_z + side_z,
                    :,
                ]
                total = total + tap_row * window.astype(jnp.float32)
    return total


def conv_grad(d_grid, padded):
    planes, side_y, side_z = (d_grid.shape[1], d_grid.shape[2], d_grid.shape[3])
    d_float = d_grid.astype(jnp.float32)
    collected = []
    for shift_x in range(3):
        for shift_y in range(3):
            for shift_z in range(3):
                window = padded[
                    :,
                    shift_x : shift_x + planes,
                    shift_y : shift_y + side_y,
                    shift_z : shift_z + side_z,
                    :,
                ]
                collected.append(jnp.sum(d_float * window.astype(jnp.float32), axis=(0, 1, 2, 3)))
    return jnp.stack(collected)


def per_device(tokens, grad_out, gain, up_weight, down_weight, conv_taps):
    feat_all, cot_all, gain_all = (
        lax.all_gather(tokens, "fsdp", axis=4, tiled=True),
        lax.all_gather(grad_out, "fsdp", axis=4, tiled=True),
        lax.all_gather(gain.astype(jnp.bfloat16), "fsdp", axis=0, tiled=True).astype(gain.dtype),
    )
    up_all, down_all = (
        lax.all_gather(up_weight, "seq", axis=0, tiled=True),
        lax.all_gather(down_weight, "seq", axis=1, tiled=True),
    )
    snaps, planes, side_y, side_z, width = feat_all.shape
    share = tokens.shape[4]
    hidden = up_all.shape[1]
    rows = snaps * planes * side_y * side_z
    contract_cols = (((1,), (1,)), ((), ()))
    contract_rows = (((0,), (0,)), ((), ()))
    flat = feat_all.reshape(rows, width).astype(jnp.float32)
    inverse = lax.rsqrt(jnp.mean(flat * flat, axis=1, keepdims=True) + epsilon)
    normed_hat = flat * inverse
    normed = (normed_hat * gain_all).astype(jnp.bfloat16)
    lifted = jnp.dot(normed, up_all, preferred_element_type=jnp.float32).astype(jnp.bfloat16)
    grid = lifted.reshape(snaps, planes, side_y, side_z, hidden)
    padded = pad_sides(with_halo(grid, (("seq", 1),), 1))
    preact = conv_apply(padded, conv_taps, False)
    value, slope = gelu_pair(preact)
    active = value.astype(jnp.bfloat16).reshape(rows, hidden)
    partial_value = jnp.dot(active, down_all, preferred_element_type=jnp.float32)
    branch = lax.psum_scatter(
        partial_value.astype(jnp.bfloat16), "fsdp", scatter_dimension=1, tiled=True
    ).astype(jnp.float32)
    own_flat = tokens.reshape(rows, share).astype(jnp.float32)
    mixed = (own_flat + branch).astype(jnp.bfloat16).reshape(tokens.shape)
    cot_flat = cot_all.reshape(rows, width)
    d_active = lax.dot_general(
        cot_flat, down_all, contract_cols, preferred_element_type=jnp.float32
    )
    d_preact = (d_active * slope.reshape(rows, hidden)).astype(jnp.bfloat16)
    d_grid = d_preact.reshape(snaps, planes, side_y, side_z, hidden)
    d_padded = pad_sides(with_halo(d_grid, (("seq", 1),), 1))
    d_lifted = conv_apply(d_padded, conv_taps, True).astype(jnp.bfloat16).reshape(rows, hidden)
    conv_term = conv_grad(d_grid, padded)
    term_down = lax.dot_general(active, cot_flat, contract_rows, preferred_element_type=jnp.float32)
    term_up = lax.dot_general(normed, d_lifted, contract_rows, preferred_element_type=jnp.float32)
    d_norm_part = lax.dot_general(
        d_lifted, up_all, contract_cols, preferred_element_type=jnp.float32
    )
    own_hat = own_flat * inverse
    d_whole = lax.psum(d_norm_part.astype(jnp.bfloat16), "fsdp").astype(jnp.float32)
    row_total = jnp.sum(d_whole * gain_all * normed_hat, axis=1, keepdims=True)
    d_norm = lax.dynamic_slice_in_dim(d_whole, lax.axis_index("fsdp") * share, share, 1)
    d_hat = d_norm * gain
    cot_own = grad_out.reshape(rows, share).astype(jnp.float32)
    grad_tokens = (
        (cot_own + inverse * (d_hat - own_hat * row_total / width))
        .astype(jnp.bfloat16)
        .reshape(tokens.shape)
    )
    gain_term = jnp.sum(d_norm * own_hat, axis=0)
    grad_conv, grad_gain = (
        lax.psum(conv_term.astype(jnp.bfloat16), ("dp", "seq")).astype(jnp.float32),
        lax.psum(gain_term.astype(jnp.bfloat16), ("dp", "seq")).astype(jnp.float32),
    )
    seq_count = lax.axis_size("seq")
    dp_count = lax.axis_size("dp")
    piece = width // (seq_count * dp_count)
    up_order = (
        term_up.reshape(seq_count, dp_count, piece, hidden)
        .transpose(1, 0, 2, 3)
        .reshape(width, hidden)
    )
    down_order = (
        term_down.reshape(hidden, seq_count, dp_count, piece)
        .transpose(0, 2, 1, 3)
        .reshape(hidden, width)
    )
    up_summed, down_summed = (
        lax.psum_scatter(
            up_order.astype(jnp.bfloat16), ("dp", "seq"), scatter_dimension=0, tiled=True
        ).astype(jnp.float32),
        lax.psum_scatter(
            down_order.astype(jnp.bfloat16), ("dp", "seq"), scatter_dimension=1, tiled=True
        ).astype(jnp.float32),
    )
    grad_up, grad_down = (
        lax.all_gather(up_summed.astype(jnp.bfloat16), "dp", axis=0, tiled=True),
        lax.all_gather(down_summed.astype(jnp.bfloat16), "dp", axis=1, tiled=True),
    )
    return (mixed, grad_tokens, grad_up, grad_down, grad_conv, grad_gain)


def solution(mesh):
    return jax.shard_map(
        per_device,
        mesh=mesh,
        in_specs=(
            P("dp", "seq", None, None, "fsdp"),
            P("dp", "seq", None, None, "fsdp"),
            P("fsdp"),
            P("seq", "fsdp"),
            P("fsdp", "seq"),
            P(None, "fsdp"),
        ),
        out_specs=(
            P("dp", "seq", None, None, "fsdp"),
            P("dp", "seq", None, None, "fsdp"),
            P("seq", "fsdp"),
            P("fsdp", "seq"),
            P(None, "fsdp"),
            P("fsdp"),
        ),
        check_vma=False,
    )
```

profile of v0, /device:TPU:0, one launch (start us, length us, event | category | flops | bytes accessed | tf_op | source)
XLA Modules:
  0.0 696.1 jit_solution(17265464418220208326)
XLA Ops:
  7.2 0.0 all-gather.8.cloned.1.call-start
  7.2 0.7 all-gather.8.cloned.1.call-update
  7.9 0.0 all-gather.10.cloned.1.call-start
  7.9 0.7 all-gather.10.cloned.1.call-update
  8.6 0.0 all-gather.14.cloned.1.call-start
  8.7 0.7 all-gather.14.cloned.1.call-update
  9.4 0.0 all-gather.12.cloned.1.call-start
  9.4 0.5 all-gather.12.cloned.1.call-update
  10.0 0.0 reduce-scatter.8.cloned.1.call-start
  10.0 0.7 convert_element_type.315
  10.7 12.0 %all-gather = bf16[8,1,512]{2,1,0:T(2,128)(2,1)S(1)} all-gather(bf16[1,1,512]{2,1,0:T(2,128)(2,1)S(1)} %reshape.198), channel_id=1, replica_groups=mesh['dp'=2,'fsdp'=8,'seq'=8] {'fsdp'}, dimensions={0}, use_global_device_ids=true | all-gather | bytes 9216 | tf_op jit(solution)/shard_map/all_gather | solution.py:84
  22.7 1.4 fusion.89
  24.3 13.0 %all-gather.8.cloned.1.call-done = bf16[1,4,8,8,4096]{4,3,2,1,0:T(8,128)(2,1)} async-done(((bf16[1,4,8,8,512]{4,3,2,1,0:T(8,128)(2,1)}), bf16[1,4,8,8,4096]{4,3,2,1,0:T(8,128)(2,1)}) %all-gather.8.cloned.1.call-update) | async-done | bytes 2097168 | tf_op jit(solution)/shard_map/all_gather | solution.py:82
  37.3 2.1 multiply_reduce_fusion.1
  39.4 0.1 rsqrt.12
  39.5 2.2 multiply_convert_fusion
  41.8 107.2 %all-gather.10.cloned.1.call-done = bf16[4096,1024]{1,0:T(8,128)(2,1)} async-done(((bf16[512,1024]{1,0:T(8,128)(2,1)}), bf16[4096,1024]{1,0:T(8,128)(2,1)}) %all-gather.10.cloned.1.call-update) | async-done | bytes 8388624 | tf_op jit(solution)/shard_map/all_gather | solution.py:87
  149.0 5.7 convolution_convert_fusion.2
  154.8 2.2 collective-permute-start
  157.0 1.3 collective-permute-start.1
  158.3 1.0 fusion.90
  159.4 14.2 %all-gather.14.cloned.1.call-done = bf16[1,4,8,8,4096]{4,3,2,1,0:T(8,128)(2,1)} async-done(((bf16[1,4,8,8,512]{4,3,2,1,0:T(8,128)(2,1)}), bf16[1,4,8,8,4096]{4,3,2,1,0:T(8,128)(2,1)}) %all-gather.14.cloned.1.call-update) | async-done | bytes 2097168 | tf_op jit(solution)/shard_map/all_gather | solution.py:83
  173.6 4.1 copy.21
  177.6 0.8 select_maximum_fusion.2
  178.6 5.2 fusion.35
  183.8 0.3 multiply_convert_fusion.1
  184.2 5.5 convert_bitcast_fusion
  189.7 8.0 %copy.22 = bf16[1024,2,8,256]{0,3,2,1:T(8,128)(2,1)} copy(bf16[1024,2,8,256]{0,3,1,2:T(8,128)(2,1)} %convert_bitcast_fusion) | data formatting | bytes 16777216 | tf_op jit(solution)/shard_map/convert_element_type | solution.py:160
  197.7 0.2 reduce-scatter.6.cloned.1.call-start
  197.9 98.7 %all-gather.12.cloned.1.call-done = bf16[1024,4096]{1,0:T(8,128)(2,1)} async-done(((bf16[1024,512]{1,0:T(8,128)(2,1)}), bf16[1024,4096]{1,0:T(8,128)(2,1)}) %all-gather.12.cloned.1.call-update) | async-done | bytes 8388624 | tf_op jit(solution)/shard_map/all_gather | solution.py:88
  296.6 8.1 %fusion.71 = (bf16[1024]{0:T(1024)(128)(2,1)}, bf16[1024]{0:T(1024)(128)(2,1)}, bf16[1024]{0:T(1024)(128)(2,1)}, bf16[1024]{0:T(1024)(128)(2,1)}, bf16[1024]{0:T...) fusion(bf16[1,1,8,8,1024]{4,3,2,1,0:T(8,128)(2,1)S(1)} %collect, ...), kind=kOutput, calls=%fused_computation.144 | convolution fusion | flops 2156126208 | bytes 16007168 | tf_op jit(solution)/shard_map/dot_general | solution.py:113
  304.8 3.1 collective-permute-start.2
  307.9 1.3 collective-permute-start.3
  309.2 4.1 copy.26
  313.2 0.5 collective-permute-done.2
  313.7 4.4 collective-permute-done.3
  318.1 0.8 select_maximum_fusion
  318.9 4.8 fusion.76
  323.8 0.8 copy-done.6
  324.6 5.5 convert_bitcast_fusion.1
  330.1 8.0 %copy.20 = bf16[2,8,256,1024]{3,2,1,0:T(8,128)(2,1)} copy(bf16[2,8,256,1024]{3,2,0,1:T(8,128)(2,1)} %convert_bitcast_fusion.1) | data formatting | bytes 16777216 | tf_op jit(solution)/shard_map/convert_element_type | solution.py:157
  338.1 0.0 reduce-scatter.6.cloned.1.call-update
  338.1 0.0 all-reduce.5.cloned.1.call-start
  338.2 7.4 %convolution_convert_fusion = bf16[256,4096]{1,0:T(8,128)(2,1)} fusion(bf16[256,1024]{1,0:T(8,128)(2,1)} %bitcast.122, bf16[4096,1024]{1,0:T(8,128)(2,1)} %all-gather.10.cloned.1.call-done), kind=kOutput, calls=%fused_computation.33 | convolution fusion | flops 2148532224 | bytes 11010048 | tf_op jit(solution)/shard_map/dot_general | solution.py:123
  345.6 0.0 all-reduce.5.cloned.1.call-update
  345.6 0.3 reduce-scatter.4.cloned.1.call-start
  345.9 7.3 %convolution_convert_fusion.1 = bf16[256,4096]{1,0:T(8,128)(2,1)} fusion(bf16[256,1024]{1,0:T(8,128)(2,1)} %bitcast.120, bf16[1024,4096]{1,0:T(8,128)(2,1)} %all-gather.12.cloned.1.call-done), kind=kOutput, calls=%fused_computation.34 | convolution fusion | flops 2148532224 | bytes 11010048 | tf_op jit(solution)/shard_map/dot_general | solution.py:106
  353.2 0.0 all-gather.18.cloned.1.call-start
  353.2 44.6 %reduce-scatter.8.cloned.1.call-done = bf16[1024,256]{0,1:T(8,128)(2,1)} async-done(((bf16[1024,4096]{0,1:T(8,128)(2,1)}), bf16[1024,256]{0,1:T(8,128)(2,1)}) %reduce-scatter.8.cloned.1.call-update) | async-done | bytes 524304 | tf_op jit(solution)/shard_map/reduce_scatter | solution.py:159
  397.8 0.0 all-gather.16.cloned.1.call-start
  397.9 105.9 %reduce-scatter.6.cloned.1.call-done = bf16[256,1024]{1,0:T(8,128)(2,1)} async-done(((bf16[4096,1024]{1,0:T(8,128)(2,1)}), bf16[256,1024]{1,0:T(8,128)(2,1)}) %reduce-scatter.6.cloned.1.call-update) | async-done | bytes 524304 | tf_op jit(solution)/shard_map/reduce_scatter | solution.py:156
  503.9 2.7 fusion.75
  506.9 0.2 multiply_reduce_fusion.2
  507.3 0.2 stack.139
  507.6 62.7 %all-reduce.5.cloned.1.call-done = bf16[256,4096]{1,0:T(8,128)(2,1)} async-done(((bf16[256,4096]{1,0:T(8,128)(2,1)}), bf16[256,4096]{1,0:T(8,128)(2,1)}) %all-reduce.5.cloned.1.call-update) | async-done | bytes 2097168 | tf_op jit(solution)/shard_map/psum | solution.py:127
  570.3 4.2 convert_element_type.382
  574.5 1.0 multiply_reduce_fusion
  575.5 30.4 %reduce-scatter.4.cloned.1.call-done = bf16[256,512]{1,0:T(8,128)(2,1)} async-done(((bf16[256,4096]{1,0:T(8,128)(2,1)}), bf16[256,512]{1,0:T(8,128)(2,1)}) %reduce-scatter.4.cloned.1.call-update) | async-done | bytes 262160 | tf_op jit(solution)/shard_map/reduce_scatter | solution.py:107
  605.8 2.2 fusion.84
  608.1 75.4 %all-reduce.2 = (bf16[27,1024]{1,0:T(8,128)(2,1)S(1)}, bf16[512]{0:T(512)(128)(2,1)S(1)}) all-reduce(bf16[27,1024]{1,0:T(8,128)(2,1)S(1)} %stack.139, bf16[512]{0:T(512)(128)(2,1)S(1)} %get-tuple-element.54), channel_id=1, replica_groups=mesh['dp'=2,'fsdp'=8,'seq'=8] {'dp','seq'}, use_global_device_ids=true, to_apply=%region_33.34 | all-reduce | flops 28160 | bytes 112640 | tf_op jit(solution)/shard_map/psum | solution.py:139
  683.4 0.7 convert_element_type.392
  684.1 0.6 convert_element_type.394
  684.7 2.3 copy.23
  687.0 2.3 copy.29
  (133 shorter events, 0.5 us)
Async XLA Ops:
  7.2 30.2 %all-gather.8.cloned.1.call-start = ((), (), s32[]{:S(2)}) async-start(), calls=%async_computation.3 | async-start | bytes 2359296 | tf_op jit(solution)/shard_map/all_gather | solution.py:82
  7.9 141.1 %all-gather.10.cloned.1.call-start = ((), (), s32[]{:S(2)}) async-start(), calls=%async_computation.4 | async-start | bytes 9437184 | tf_op jit(solution)/shard_map/all_gather | solution.py:87
  8.6 164.9 %all-gather.14.cloned.1.call-start = ((), (), s32[]{:S(2)}) async-start(), calls=%async_computation.7 | async-start | bytes 2359296 | tf_op jit(solution)/shard_map/all_gather | solution.py:83
  9.4 287.3 %all-gather.12.cloned.1.call-start = ((), (), s32[]{:S(2)}) async-start(), calls=%async_computation.5 | async-start | bytes 9437184 | tf_op jit(solution)/shard_map/all_gather | solution.py:88
  10.0 387.9 %reduce-scatter.8.cloned.1.call-start = ((), (), s32[]{:S(2)}) async-start(), calls=%async_computation.11 | async-start | bytes 8912896 | tf_op jit(solution)/shard_map/reduce_scatter | solution.py:159
  24.1 154.2 %copy-start.9 = (f32[1,1024]{1,0:T(1,128)}, f32[1,1024]{1,0:T(1,128)S(1)}, u32[]{:S(2)}) copy-start(f32[1,1024]{1,0:T(1,128)S(1)} %get-tuple-element.61) | copy-start | bytes 12292
  24.2 154.2 %copy-start.10 = (f32[1,1024]{1,0:T(1,128)}, f32[1,1024]{1,0:T(1,128)S(1)}, u32[]{:S(2)}) copy-start(f32[1,1024]{1,0:T(1,128)S(1)} %get-tuple-element.62) | copy-start | bytes 12292
  24.2 154.2 %copy-start.11 = (f32[1,1024]{1,0:T(1,128)}, f32[1,1024]{1,0:T(1,128)S(1)}, u32[]{:S(2)}) copy-start(f32[1,1024]{1,0:T(1,128)S(1)} %get-tuple-element.63) | copy-start | bytes 12292
  24.2 154.2 %copy-start.12 = (f32[1,1024]{1,0:T(1,128)}, f32[1,1024]{1,0:T(1,128)S(1)}, u32[]{:S(2)}) copy-start(f32[1,1024]{1,0:T(1,128)S(1)} %get-tuple-element.64) | copy-start | bytes 12292
  24.2 154.2 %copy-start.13 = (f32[1,1024]{1,0:T(1,128)}, f32[1,1024]{1,0:T(1,128)S(1)}, u32[]{:S(2)}) copy-start(f32[1,1024]{1,0:T(1,128)S(1)} %get-tuple-element.65) | copy-start | bytes 12292
  24.2 154.2 %copy-start.14 = (f32[1,1024]{1,0:T(1,128)}, f32[1,1024]{1,0:T(1,128)S(1)}, u32[]{:S(2)}) copy-start(f32[1,1024]{1,0:T(1,128)S(1)} %get-tuple-element.66) | copy-start | bytes 12292
  24.2 154.2 %copy-start.15 = (f32[1,1024]{1,0:T(1,128)}, f32[1,1024]{1,0:T(1,128)S(1)}, u32[]{:S(2)}) copy-start(f32[1,1024]{1,0:T(1,128)S(1)} %get-tuple-element.67) | copy-start | bytes 12292
  24.2 154.2 %copy-start.16 = (f32[1,1024]{1,0:T(1,128)}, f32[1,1024]{1,0:T(1,128)S(1)}, u32[]{:S(2)}) copy-start(f32[1,1024]{1,0:T(1,128)S(1)} %get-tuple-element.68) | copy-start | bytes 12292
  24.2 154.2 %copy-start.17 = (f32[1,1024]{1,0:T(1,128)}, f32[1,1024]{1,0:T(1,128)S(1)}, u32[]{:S(2)}) copy-start(f32[1,1024]{1,0:T(1,128)S(1)} %get-tuple-element.69) | copy-start | bytes 12292
  24.2 154.2 %copy-start.18 = (f32[1,1024]{1,0:T(1,128)}, f32[1,1024]{1,0:T(1,128)S(1)}, u32[]{:S(2)}) copy-start(f32[1,1024]{1,0:T(1,128)S(1)} %get-tuple-element.70) | copy-start | bytes 12292
  24.2 154.2 %copy-start.19 = (f32[1,1024]{1,0:T(1,128)}, f32[1,1024]{1,0:T(1,128)S(1)}, u32[]{:S(2)}) copy-start(f32[1,1024]{1,0:T(1,128)S(1)} %get-tuple-element.71) | copy-start | bytes 12292
  24.3 154.2 %copy-start.20 = (f32[1,1024]{1,0:T(1,128)}, f32[1,1024]{1,0:T(1,128)S(1)}, u32[]{:S(2)}) copy-start(f32[1,1024]{1,0:T(1,128)S(1)} %get-tuple-element.72) | copy-start | bytes 12292
  24.3 154.2 %copy-start.21 = (f32[1,1024]{1,0:T(1,128)}, f32[1,1024]{1,0:T(1,128)S(1)}, u32[]{:S(2)}) copy-start(f32[1,1024]{1,0:T(1,128)S(1)} %get-tuple-element.73) | copy-start | bytes 12292
  24.3 154.2 %copy-start.22 = (f32[1,1024]{1,0:T(1,128)}, f32[1,1024]{1,0:T(1,128)S(1)}, u32[]{:S(2)}) copy-start(f32[1,1024]{1,0:T(1,128)S(1)} %get-tuple-element.74) | copy-start | bytes 12292
  24.3 154.2 %copy-start.23 = (f32[1,1024]{1,0:T(1,128)}, f32[1,1024]{1,0:T(1,128)S(1)}, u32[]{:S(2)}) copy-start(f32[1,1024]{1,0:T(1,128)S(1)} %get-tuple-element.75) | copy-start | bytes 12292
  24.3 154.2 %copy-start.24 = (f32[1,1024]{1,0:T(1,128)}, f32[1,1024]{1,0:T(1,128)S(1)}, u32[]{:S(2)}) copy-start(f32[1,1024]{1,0:T(1,128)S(1)} %get-tuple-element.76) | copy-start | bytes 12292
  24.3 154.2 %copy-start.25 = (f32[1,1024]{1,0:T(1,128)}, f32[1,1024]{1,0:T(1,128)S(1)}, u32[]{:S(2)}) copy-start(f32[1,1024]{1,0:T(1,128)S(1)} %get-tuple-element.77) | copy-start | bytes 12292
  24.3 154.2 %copy-start.26 = (f32[1,1024]{1,0:T(1,128)}, f32[1,1024]{1,0:T(1,128)S(1)}, u32[]{:S(2)}) copy-start(f32[1,1024]{1,0:T(1,128)S(1)} %get-tuple-element.78) | copy-start | bytes 12292
  24.3 154.2 %copy-start.27 = (f32[1,1024]{1,0:T(1,128)}, f32[1,1024]{1,0:T(1,128)S(1)}, u32[]{:S(2)}) copy-start(f32[1,1024]{1,0:T(1,128)S(1)} %get-tuple-element.79) | copy-start | bytes 12292
  39.5 115.2 %copy-start.36 = (f32[256]{0:T(256)}, f32[256]{0:T(256)S(1)}, u32[]{:S(2)}) copy-start(f32[256]{0:T(256)S(1)} %rsqrt.12) | copy-start | bytes 3076
  41.7 113.0 %copy-start.4 = (bf16[256,4096]{1,0:T(8,128)(2,1)}, bf16[256,4096]{1,0:T(8,128)(2,1)S(1)}, u32[]{:S(2)}) copy-start(bf16[256,4096]{1,0:T(8,128)(2,1)S(1)} %multiply_convert_fusion) | copy-start | bytes 6291460
  154.8 22.9 %collective-permute-start = (bf16[1,1,8,8,1024]{4,3,2,1,0:T(8,128)(2,1)S(1)}, bf16[1,1,8,8,1024]{4,3,2,1,0:T(8,128)(2,1)S(1)}, u32[]{:S(2)}, u32[]{:S(2)}) collective-permute-start(bf16[1,1,8,8,1024]{4,3,2,1,0:T(8,128)(2,1)S(1)} %get-tuple-element.58), channel_id=1, source_target_pairs={{0,1},{1,2},{2,3},{3,4},{4,5},{5,6},{6,7},{8,9},{9,10},{10,11},{11... | collective-permute-start | bytes 393224 | tf_op jit(solution)/shard_map/ppermute | solution.py:16
  157.0 20.7 %collective-permute-start.1 = (bf16[1,1,8,8,1024]{4,3,2,1,0:T(8,128)(2,1)S(1)}, bf16[1,1,8,8,1024]{4,3,2,1,0:T(8,128)(2,1)S(1)}, u32[]{:S(2)}, u32[]{:S(2)}) collective-permute-start(bf16[1,1,8,8,1024]{4,3,2,1,0:T(8,128)(2,1)S(1)} %get-tuple-element.59), channel_id=1, source_target_pairs={{1,0},{2,1},{3,2},{4,3},{5,4},{6,5},{7,6},{9,8},{10,9},{11,10},{12... | collective-permute-start | bytes 393224 | tf_op jit(solution)/shard_map/ppermute | solution.py:19
  159.3 24.5 %copy-start.28 = (f32[1,1024]{1,0:T(1,128)}, f32[1,1024]{1,0:T(1,128)S(1)}, u32[]{:S(2)}) copy-start(f32[1,1024]{1,0:T(1,128)S(1)} %get-tuple-element.80) | copy-start | bytes 12292
  159.3 24.5 %copy-start.29 = (f32[1,1024]{1,0:T(1,128)}, f32[1,1024]{1,0:T(1,128)S(1)}, u32[]{:S(2)}) copy-start(f32[1,1024]{1,0:T(1,128)S(1)} %get-tuple-element.81) | copy-start | bytes 12292
  159.3 24.5 %copy-start.30 = (f32[1,1024]{1,0:T(1,128)}, f32[1,1024]{1,0:T(1,128)S(1)}, u32[]{:S(2)}) copy-start(f32[1,1024]{1,0:T(1,128)S(1)} %get-tuple-element.82) | copy-start | bytes 12292
  159.3 24.5 %copy-start.31 = (f32[1,1024]{1,0:T(1,128)}, f32[1,1024]{1,0:T(1,128)S(1)}, u32[]{:S(2)}) copy-start(f32[1,1024]{1,0:T(1,128)S(1)} %get-tuple-element.83) | copy-start | bytes 12292
  159.3 24.5 %copy-start.32 = (f32[1,1024]{1,0:T(1,128)}, f32[1,1024]{1,0:T(1,128)S(1)}, u32[]{:S(2)}) copy-start(f32[1,1024]{1,0:T(1,128)S(1)} %get-tuple-element.84) | copy-start | bytes 12292
  159.3 24.5 %copy-start.33 = (f32[1,1024]{1,0:T(1,128)}, f32[1,1024]{1,0:T(1,128)S(1)}, u32[]{:S(2)}) copy-start(f32[1,1024]{1,0:T(1,128)S(1)} %get-tuple-element.85) | copy-start | bytes 12292
  159.3 24.5 %copy-start.34 = (f32[1,1024]{1,0:T(1,128)}, f32[1,1024]{1,0:T(1,128)S(1)}, u32[]{:S(2)}) copy-start(f32[1,1024]{1,0:T(1,128)S(1)} %get-tuple-element.86) | copy-start | bytes 12292
  159.3 24.5 %copy-start.35 = (f32[1,1024]{1,0:T(1,128)}, f32[1,1024]{1,0:T(1,128)S(1)}, u32[]{:S(2)}) copy-start(f32[1,1024]{1,0:T(1,128)S(1)} %get-tuple-element.87) | copy-start | bytes 12292
  178.6 5.6 copy-start.2
  184.1 5.6 copy-start.5
  197.7 306.1 %reduce-scatter.6.cloned.1.call-start = ((), (), s32[]{:S(2)}) async-start(), calls=%async_computation.9 | async-start | bytes 8912896 | tf_op jit(solution)/shard_map/reduce_scatter | solution.py:156
  304.8 9.0 %collective-permute-start.2 = (bf16[1,1,8,8,1024]{4,3,2,1,0:T(8,128)(2,1)S(1)}, bf16[1,1,8,8,1024]{4,3,2,1,0:T(8,128)(2,1)S(1)}, u32[]{:S(2)}, u32[]{:S(2)}) collective-permute-start(bf16[1,1,8,8,1024]{4,3,2,1,0:T(8,128)(2,1)S(1)} %get-tuple-element.56), channel_id=1, source_target_pairs={{0,1},{1,2},{2,3},{3,4},{4,5},{5,6},{6,7},{8,9},{9,10},{10,11},{11... | collective-permute-start | bytes 393224 | tf_op jit(solution)/shard_map/ppermute | solution.py:16
  307.9 10.3 %collective-permute-start.3 = (bf16[1,1,8,8,1024]{4,3,2,1,0:T(8,128)(2,1)S(1)}, bf16[1,1,8,8,1024]{4,3,2,1,0:T(8,128)(2,1)S(1)}, u32[]{:S(2)}, u32[]{:S(2)}) collective-permute-start(bf16[1,1,8,8,1024]{4,3,2,1,0:T(8,128)(2,1)S(1)} %get-tuple-element.57), channel_id=1, source_target_pairs={{1,0},{2,1},{3,2},{4,3},{5,4},{6,5},{7,6},{9,8},{10,9},{11,10},{12... | collective-permute-start | bytes 393224 | tf_op jit(solution)/shard_map/ppermute | solution.py:19
  318.9 5.7 copy-start.1
  323.8 0.8 copy-start.6
  338.1 232.2 %all-reduce.5.cloned.1.call-start = ((), (), s32[]{:S(2)}) async-start(), calls=%async_computation.8 | async-start | bytes 4194304 | tf_op jit(solution)/shard_map/psum | solution.py:127
  345.6 260.2 %reduce-scatter.4.cloned.1.call-start = ((), (), s32[]{:S(2)}) async-start(), calls=%async_computation.6 | async-start | bytes 2359296 | tf_op jit(solution)/shard_map/reduce_scatter | solution.py:107
  353.2 331.5 %all-gather.18.cloned.1.call-start = ((), (), s32[]{:S(2)}) async-start(), calls=%async_computation.12 | async-start | bytes 1572864 | tf_op jit(solution)/shard_map/all_gather | solution.py:165
  397.8 289.1 %all-gather.16.cloned.1.call-start = ((), (), s32[]{:S(2)}) async-start(), calls=%async_computation.10 | async-start | bytes 1572864 | tf_op jit(solution)/shard_map/all_gather | solution.py:164
  503.9 3.3 copy-start.46
  503.9 3.3 copy-start.45
  503.9 3.3 copy-start.44
  503.9 3.3 copy-start.43
  503.9 3.3 copy-start.42
  503.9 3.3 copy-start.41
  503.9 3.4 copy-start.40
  503.9 3.4 copy-start.39
  506.7 67.8 %copy-start = (bf16[1,4,8,8,4096]{4,3,2,1,0:T(8,128)(2,1)S(1)}, bf16[1,4,8,8,4096]{4,3,2,1,0:T(8,128)(2,1)}, u32[]{:S(2)}) copy-start(bf16[1,4,8,8,4096]{4,3,2,1,0:T(8,128)(2,1)} %all-gather.8.cloned.1.call-done) | copy-start | bytes 6291460
  506.7 67.8 %copy-start.37 = (f32[256]{0:T(256)S(1)}, f32[256]{0:T(256)}, u32[]{:S(2)}) copy-start(f32[256]{0:T(256)} %copy-done.36) | copy-start | bytes 3076
  507.5 98.3 %copy-start.7 = (bf16[1,4,8,8,512]{4,3,2,1,0:T(8,128)(2,1)S(1)}, bf16[1,4,8,8,512]{4,3,2,1,0:T(8,128)(2,1)}, u32[]{:S(2)}) copy-start(bf16[1,4,8,8,512]{4,3,2,1,0:T(8,128)(2,1)} %param.6) | copy-start | bytes 786436
  507.5 98.3 %copy-start.8 = (bf16[1,4,8,8,512]{4,3,2,1,0:T(8,128)(2,1)S(1)}, bf16[1,4,8,8,512]{4,3,2,1,0:T(8,128)(2,1)}, u32[]{:S(2)}) copy-start(bf16[1,4,8,8,512]{4,3,2,1,0:T(8,128)(2,1)} %param.7) | copy-start | bytes 786436
  507.6 98.3 %copy-start.38 = (f32[512]{0:T(512)S(1)}, f32[512]{0:T(512)}, u32[]{:S(2)}) copy-start(f32[512]{0:T(512)} %param.8) | copy-start | bytes 6148
  570.3 4.2 copy-start.3
Sparse Core Ops, SparseCore 0:
  9.7 27.5 all-gather.7
  39.7 109.2 all-gather.9
  150.7 22.8 all-gather.13
  175.6 121.0 all-gather.11
  298.9 98.8 reduce-scatter.7
  400.1 103.7 reduce-scatter.5
  506.2 64.0 all-reduce.4
  572.7 33.0 reduce-scatter.3
  607.5 23.1 all-gather.17
  632.2 25.2 all-gather.15
where the time goes:
time: 697 us; the launch traced here: 696 us
  waiting for transfers between devices  484 us (69%)
  blocking collectives  87.4 us (13%)
  matrix products  39.5 us (6%)
  local copies, waits for them, and re-layouts  32.6 us (5%)
  other arithmetic  28.4 us (4%)
  between operations  15.1 us (2%)
  starting transfers between devices  8.67 us (1%)
    all_gather x1, waiting for transfers between devices, per_device(): lax.all_gather(up_weight, 'seq', axis=0, tiled=True)  107 us
    reduce_scatter x1, waiting for transfers between devices, per_device(): lax.psum_scatter(up_order.astype(jnp.bfloat16), ('dp', 'seq'), scatter_di...  106 us
    all_gather x1, waiting for transfers between devices, per_device(): lax.all_gather(down_weight, 'seq', axis=1, tiled=True)  98.7 us
    psum x1, blocking collectives, per_device(): lax.psum(conv_term.astype(jnp.bfloat16), ('dp', 'seq')).astype(jnp.float32)  75.4 us
    psum x1, waiting for transfers between devices, per_device(): lax.psum(d_norm_part.astype(jnp.bfloat16), 'fsdp').astype(jnp.float32)  62.7 us
    reduce_scatter x1, waiting for transfers between devices, per_device(): lax.psum_scatter(down_order.astype(jnp.bfloat16), ('dp', 'seq'), scatter_...  44.6 us
    reduce_scatter x1, waiting for transfers between devices, per_device(): lax.psum_scatter(partial_value.astype(jnp.bfloat16), 'fsdp', scatter_dime...  30.4 us
    all_gather x1, waiting for transfers between devices, per_device(): lax.all_gather(grad_out, 'fsdp', axis=4, tiled=True)  14.2 us
  transfers between devices with their start and end apart: 14, of which 10 were waited for; matrix products, arithmetic and copies ran while one was open for 14% of the time, Pallas kernels for 0%

commit v1 on v0

v1 whole, which is shorter than its diff:
```python
import functools

import jax
import jax.numpy as jnp
from jax import lax
from jax.experimental import pallas as pl
from jax.experimental.pallas import tpu as pltpu
from jax.sharding import PartitionSpec as P

MESH = pl.DeviceIdType.MESH
gelu_scale = 0.7978845608028654
gelu_cubic = 0.044715
epsilon = 1e-06
B = 512


class Place:
    def __init__(self):
        self.zl = lax.axis_index("dp")
        self.f = lax.axis_index("fsdp")
        self.s = lax.axis_index("seq")
        self.x, self.c = lax.div(self.f, 2), lax.rem(self.f, 2)
        self.zh, self.y = lax.div(self.s, 4), lax.rem(self.s, 4)
        self.xs = [lax.rem(self.x + k, 4) for k in range(4)]
        self.ys = [lax.rem(self.y + k, 4) for k in range(4)]
        self.other_zl = {"dp": 1 - self.zl}
        self.other_core = {"fsdp": self.feat(0, 1)}
        self.x_up, self.x_down = {"fsdp": self.feat(1)}, {"fsdp": self.feat(3)}
        self.other_zh = {"seq": self.slab(0, 1)}
        self.y_up, self.y_down = {"seq": self.slab(1)}, {"seq": self.slab(3)}

    def feat(self, k, flip=0):
        return self.xs[k] * 2 + (1 - self.c if flip else self.c)

    def slab(self, k, flip=0):
        return (1 - self.zh if flip else self.zh) * 4 + self.ys[k]

    def partners(self):
        return [self.other_zl, self.other_core, self.x_up, self.x_down, self.other_zh, self.y_up, self.y_down]


class Wires:
    def __init__(self, send, recv):
        self.send, self.recv, self.copies = send, recv, []

    def start(self, src, dst, where):
        i = len(self.copies)
        copy = pltpu.make_async_remote_copy(
            src_ref=src, dst_ref=dst, send_sem=self.send.at[i], recv_sem=self.recv.at[i],
            device_id=where, device_id_type=MESH,
        )
        copy.start()
        self.copies.append(copy)
        return copy

    def finish(self):
        for copy in self.copies:
            copy.wait_send()


def meet(partners):
    barrier = pltpu.get_barrier_semaphore()
    for where in partners:
        pl.semaphore_signal(barrier, inc=1, device_id=where, device_id_type=MESH)
    pl.semaphore_wait(barrier, len(partners))


class WeightGather:
    def __init__(self, me, wires, own, buf):
        self.me, self.wires, self.own, self.buf = me, wires, own, buf

    def start_z(self):
        self.z = self.wires.start(self.own, self.buf.at[self.me.s], self.me.other_zh)

    def start_y(self):
        self.up = self.wires.start(self.own, self.buf.at[self.me.s], self.me.y_up)
        self.down = self.wires.start(self.own, self.buf.at[self.me.s], self.me.y_down)

    def forward(self, flip):
        me, buf = self.me, self.buf
        below, above = me.slab(3, flip), me.slab(1, flip)
        self.up.wait_recv()
        part = buf.at[below, pl.ds(0, B // 2)]
        first = self.wires.start(part, part, me.y_up)
        self.down.wait_recv()
        part = buf.at[above, pl.ds(B // 2, B // 2)]
        return first, self.wires.start(part, part, me.y_down)

    def forward_own(self):
        self.far = self.forward(0)

    def start_other(self):
        self.z.wait_recv()
        block = self.buf.at[self.me.slab(0, 1)]
        self.up = self.wires.start(block, block, self.me.y_up)
        self.down = self.wires.start(block, block, self.me.y_down)

    def forward_other(self):
        self.far_other = self.forward(1)

    def wait_far(self):
        for copy in self.far:
            copy.wait_recv()

    def wait_far_other(self):
        for copy in self.far_other:
            copy.wait_recv()


class TokenGather:
    def __init__(self, me, wires, own, buf):
        self.me, self.wires, self.own, self.buf = me, wires, own, buf
        self.cores = []

    def rows(self, half, part=None):
        if part is None:
            return pl.ds(pl.multiple_of(half * 256, 256), 256)
        return pl.ds(pl.multiple_of(half * 256 + part * 128, 128), 128)

    def start_own(self):
        me = self.me
        dst = self.buf.at[me.f, self.rows(me.zl)]
        self.z = self.wires.start(self.own, dst, me.other_zl)
        self.ring = [self.wires.start(self.own, dst, where) for where in (me.x_up, me.x_down)]
        self.cores.append(self.wires.start(self.own, dst, me.other_core))

    def to_core(self, k, half):
        block = self.buf.at[self.me.feat(k), self.rows(half)]
        self.cores.append(self.wires.start(block, block, self.me.other_core))

    def forward(self, half):
        me, buf, ring = self.me, self.buf, self.ring
        ring[0].wait_recv()
        part = buf.at[me.feat(3), self.rows(half, 0)]
        first = self.wires.start(part, part, me.x_up)
        ring[1].wait_recv()
        part = buf.at[me.feat(1), self.rows(half, 1)]
        self.far = first, self.wires.start(part, part, me.x_down)
        self.to_core(3, half)
        self.to_core(1, half)

    def start_other(self):
        me = self.me
        self.z.wait_recv()
        block = self.buf.at[me.f, self.rows(1 - me.zl)]
        self.ring = [self.wires.start(block, block, where) for where in (me.x_up, me.x_down)]
        self.to_core(0, 1 - me.zl)

    def finish_half(self, half):
        for copy in self.far:
            copy.wait_recv()
        self.to_core(2, half)

    def wait_cores(self):
        for copy in self.cores:
            copy.wait_recv()


def gather_kernel(tok, gout, up, down, gain, T, G, U, D, N, local, send, recv):
    me = Place()
    peers = [lax.rem(me.f + k, 8) for k in range(1, 8)]
    meet(me.partners() + [{"fsdp": p} for p in peers])
    wires = Wires(send, recv)
    up_own = up.at[:, pl.ds(pl.multiple_of(me.zl * B, B), B)]
    down_own = down.at[pl.ds(pl.multiple_of(me.zl * B, B), B), :]
    u, d = WeightGather(me, wires, up_own, U), WeightGather(me, wires, down_own, D)
    t, g = TokenGather(me, wires, tok, T), TokenGather(me, wires, gout, G)
    u.start_z()
    u.start_y()
    t.start_own()
    gains = [wires.start(gain, N.at[me.f], {"fsdp": p}) for p in peers]
    own = me.rows = t.rows(me.zl)
    here = [
        pltpu.make_async_copy(src, dst, local.at[i])
        for i, (src, dst) in enumerate(
            [
                (up_own, U.at[me.s]),
                (down_own, D.at[me.s]),
                (tok, T.at[me.f, own]),
                (gout, G.at[me.f, own]),
                (gain, N.at[me.f]),
            ]
        )
    ]
    for copy in here:
        copy.start()
    d.start_z()
    t.forward(me.zl)
    t.start_other()
    g.start_own()
    u.forward_own()
    u.start_other()
    d.start_y()
    t.finish_half(me.zl)
    t.forward(1 - me.zl)
    g.forward(me.zl)
    g.start_other()
    t.finish_half(1 - me.zl)
    u.wait_far()
    u.forward_other()
    d.forward_own()
    d.start_other()
    g.finish_half(me.zl)
    g.forward(1 - me.zl)
    g.finish_half(1 - me.zl)
    u.wait_far_other()
    d.wait_far()
    d.forward_other()
    d.wait_far_other()
    t.wait_cores()
    g.wait_cores()
    for copy in gains:
        copy.wait_recv()
    for copy in here:
        copy.wait()
    wires.finish()


def gather(tok, gout, up, down, gain):
    blocks = jax.ShapeDtypeStruct((8, B, B), jnp.bfloat16)
    return pl.pallas_call(
        gather_kernel,
        out_shape=[blocks, blocks, blocks, blocks, jax.ShapeDtypeStruct((8, 8, B), jnp.float32)],
        in_specs=[pl.BlockSpec(memory_space=pl.ANY)] * 5,
        out_specs=[pl.BlockSpec(memory_space=pl.ANY)] * 5,
        scratch_shapes=[
            pltpu.SemaphoreType.DMA((5,)),
            pltpu.SemaphoreType.DMA((72,)),
            pltpu.SemaphoreType.DMA((72,)),
        ],
        compiler_params=pltpu.CompilerParams(collective_id=0, has_side_effects=True, vmem_limit_bytes=8 << 20),
        name="gather",
    )(tok, gout, up, down, gain)


def add(*parts):
    total = parts[0].astype(jnp.float32)
    for part in parts[1:]:
        total = total + part.astype(jnp.float32)
    return total


class RowScatter:
    def __init__(self, me, wires, terms, from_core, held, from_far, from_near, to_z, from_z):
        self.me, self.wires, self.terms = me, wires, terms
        self.from_core, self.held, self.from_far, self.from_near = from_core, held, from_far, from_near
        self.to_z, self.from_z = to_z, from_z

    def start_core(self):
        me = self.me
        self.core = {}
        for k in (2, 1, 3, 0):
            self.core[k] = self.wires.start(
                self.terms.at[me.feat(k, 1)], self.from_core.at[me.xs[k]], me.other_core
            )

    def join(self, k):
        self.core[k].wait_recv()
        me = self.me
        self.held[k] = add(self.terms[me.feat(k)], self.from_core[me.xs[k]]).astype(jnp.bfloat16)

    def start_far(self):
        me = self.me
        self.join(2)
        self.far = [
            self.wires.start(self.held.at[2, pl.ds(0, 256)], self.from_far.at[0], me.x_up),
            self.wires.start(self.held.at[2, pl.ds(256, 256)], self.from_far.at[1], me.x_down),
        ]
        self.join(1)
        self.join(3)
        self.join(0)

    def start_near(self):
        me, held = self.me, self.held
        self.far[0].wait_recv()
        held[1, :256] = add(held[1, :256], self.from_far[0]).astype(jnp.bfloat16)
        first = self.wires.start(held.at[1], self.from_near.at[0], me.x_up)
        self.far[1].wait_recv()
        held[3, 256:] = add(held[3, 256:], self.from_far[1]).astype(jnp.bfloat16)
        self.near = first, self.wires.start(held.at[3], self.from_near.at[1], me.x_down)

    def start_z(self):
        me = self.me
        self.near[0].wait_recv()
        self.near[1].wait_recv()
        rows = pl.ds(pl.multiple_of((1 - me.zl) * 256, 256), 256)
        self.to_z[...] = add(self.held[0, rows], self.from_near[0, rows], self.from_near[1, rows]).astype(jnp.bfloat16)
        self.z = self.wires.start(self.to_z, self.from_z, me.other_zl)

    def result(self):
        rows = pl.ds(pl.multiple_of(self.me.zl * 256, 256), 256)
        self.z.wait_recv()
        return add(self.held[0, rows], self.from_near[0, rows], self.from_near[1, rows], self.from_z[...])

    @staticmethod
    def scratch():
        blocks = lambda *shape: pltpu.VMEM(shape, jnp.bfloat16)
        return [blocks(4, B, B), blocks(4, B, B), blocks(2, 256, B), blocks(2, B, B), blocks(256, B), blocks(256, B)]


class WeightScatter:
    def __init__(self, me, wires, terms, held, from_far, from_near, to_z, from_z):
        self.me, self.wires, self.terms, self.held = me, wires, terms, held
        self.from_far, self.from_near, self.to_z, self.from_z = from_far, from_near, to_z, from_z

    def start_far(self):
        me, y = self.me, self.me.ys
        start = self.wires.start
        self.far = [
            start(self.terms.at[y[2]], self.from_far.at[0], me.y_up),
            start(self.terms.at[4 + y[2]], self.from_far.at[1], me.y_down),
        ]
        self.near = [
            start(self.terms.at[4 + y[1]], self.from_near.at[1], me.y_up),
            start(self.terms.at[y[3]], self.from_near.at[2], me.y_down),
        ]

    def start_near(self):
        me, y = self.me, self.me.ys
        start = self.wires.start
        self.far[0].wait_recv()
        self.held[0] = add(self.terms[y[1]], self.from_far[0]).astype(jnp.bfloat16)
        self.near.append(start(self.held.at[0], self.from_near.at[0], me.y_up))
        self.far[1].wait_recv()
        self.held[1] = add(self.terms[4 + y[3]], self.from_far[1]).astype(jnp.bfloat16)
        self.near.append(start(self.held.at[1], self.from_near.at[3], me.y_down))

    def total(self, zh):
        return add(self.terms[zh * 4 + self.me.y], self.from_near[zh], self.from_near[2 + zh])

    def start_z(self):
        for copy in self.near:
            copy.wait_recv()
        self.to_z[...] = self.total(1 - self.me.zh).astype(jnp.bfloat16)
        self.z = self.wires.start(self.to_z, self.from_z, self.me.other_zh)

    def start_out(self, out):
        self.z.wait_recv()
        out[...] = (self.total(self.me.zh) + self.from_z[...].astype(jnp.float32)).astype(jnp.bfloat16)
        self.last = self.wires.start(out, out, self.me.other_zl)

    def wait_out(self):
        self.last.wait_recv()

    @staticmethod
    def scratch():
        blocks = lambda *shape: pltpu.VMEM(shape, jnp.bfloat16)
        return [blocks(2, B, B), blocks(2, B, B), blocks(4, B, B), blocks(B, B), blocks(B, B)]


def scatter_kernel(branch, norm, g_up, g_down, branch_out, norm_out, up_out, down_out, *scratch):
    me = Place()
    meet(me.partners())
    send, recv = scratch[-2:]
    wires = Wires(send, recv)
    b = RowScatter(me, wires, branch, *scratch[0:6])
    n = RowScatter(me, wires, norm, *scratch[6:12])
    dn = WeightScatter(me, wires, g_down, *scratch[12:17])
    u = WeightScatter(me, wires, g_up, *scratch[17:22])
    dn.start_far()
    b.start_core()
    b.start_far()
    b.start_near()
    n.start_core()
    dn.start_near()
    u.start_far()
    n.start_far()
    n.start_near()
    b.start_z()
    dn.start_z()
    u.start_near()
    branch_out[...] = b.result()
    n.start_z()
    dn.start_out(down_out.at[me.zl])
    norm_out[...] = n.result()
    u.start_z()
    u.start_out(up_out.at[me.zl])
    dn.wait_out()
    u.wait_out()
    wires.finish()


def scatter(branch, norm, g_up, g_down):
    f32 = jax.ShapeDtypeStruct((256, B), jnp.float32)
    pair = jax.ShapeDtypeStruct((2, B, B), jnp.bfloat16)
    return pl.pallas_call(
        scatter_kernel,
        out_shape=[f32, f32, pair, pair],
        in_specs=[pl.BlockSpec(memory_space=pltpu.VMEM)] * 4,
        out_specs=[pl.BlockSpec(memory_space=pltpu.VMEM)] * 4,
        scratch_shapes=RowScatter.scratch() * 2
        + WeightScatter.scratch() * 2
        + [pltpu.SemaphoreType.DMA((40,)), pltpu.SemaphoreType.DMA((40,))],
        compiler_params=pltpu.CompilerParams(collective_id=1, has_side_effects=True, vmem_limit_bytes=60 << 20),
        name="scatter",
    )(branch, norm, g_up, g_down)


def with_halo(block):
    count = lax.axis_size("seq")
    forward = [(i, i + 1) for i in range(count - 1)]
    backward = [(target, source) for source, target in forward]
    low = lax.ppermute(block[:, 3:4], "seq", forward)
    high = lax.ppermute(block[:, 0:1], "seq", backward)
    return jnp.concatenate([low, block, high], axis=1)


def gelu_pair(preact):
    inner = gelu_scale * (preact + gelu_cubic * preact * preact * preact)
    tangent = jnp.tanh(inner)
    value = 0.5 * preact * (1.0 + tangent)
    slope = 0.5 * (1.0 + tangent) + 0.5 * preact * (1.0 - tangent * tangent) * gelu_scale * (
        1.0 + 3.0 * gelu_cubic * preact * preact
    )
    return (value, slope)


def pad_sides(field):
    return jnp.pad(field, ((0, 0), (0, 0), (1, 1), (1, 1), (0, 0)))


def conv_apply(padded, kernel, flipped):
    total = jnp.zeros((2, 4, 8, 8, padded.shape[4]), jnp.float32)
    for index in range(27):
        a, b, c = index // 9, index // 3 % 3, index % 3
        tap_row = kernel[26 - index] if flipped else kernel[index]
        window = padded[:, a : a + 4, b : b + 8, c : c + 8, :]
        total = total + tap_row * window.astype(jnp.float32)
    return total


def conv_grad(d_grid, padded):
    d_float = d_grid.astype(jnp.float32)
    collected = []
    for index in range(27):
        a, b, c = index // 9, index // 3 % 3, index % 3
        window = padded[:, a : a + 4, b : b + 8, c : c + 8, :]
        collected.append(jnp.sum(d_float * window.astype(jnp.float32), axis=(0, 1, 2, 3)))
    return jnp.stack(collected)


def per_device(tokens, grad_out, gain, up_weight, down_weight, conv_taps):
    zl, f = lax.axis_index("dp"), lax.axis_index("fsdp")
    tok = tokens.reshape(256, B)
    gout = grad_out.reshape(256, B)
    gain_rows = jnp.broadcast_to(gain[None], (8, B))
    T, G, U, D, N = gather(tok, gout, up_weight, down_weight, gain_rows)
    gain_all = N[:, 0:1, :]
    taps = lax.dynamic_slice_in_dim(conv_taps, zl * B, B, 1)
    flat = T.astype(jnp.float32)
    inverse = lax.rsqrt(jnp.sum(flat * flat, axis=(0, 2)) / 4096.0 + epsilon)[:, None]
    normed = (flat * inverse[None] * gain_all).astype(jnp.bfloat16)
    f32 = dict(preferred_element_type=jnp.float32)
    lifted = jnp.einsum("brd,bdh->rh", normed, U, **f32).astype(jnp.bfloat16)
    padded = pad_sides(with_halo(lifted.reshape(2, 4, 8, 8, B)))
    preact = conv_apply(padded, taps, False)
    value, slope = gelu_pair(preact)
    active = value.astype(jnp.bfloat16).reshape(512, B)
    branch_term = jnp.einsum("rh,bhd->brd", active, D, **f32).astype(jnp.bfloat16)
    d_active = jnp.einsum("brd,bhd->rh", G, D, **f32)
    down_term = jnp.einsum("rh,brd->bhd", active, G, **f32).astype(jnp.bfloat16)
    d_preact = (d_active * slope.reshape(512, B)).astype(jnp.bfloat16)
    d_grid = d_preact.reshape(2, 4, 8, 8, B)
    d_padded = pad_sides(with_halo(d_grid))
    d_lifted = conv_apply(d_padded, taps, True).astype(jnp.bfloat16).reshape(512, B)
    conv_term = conv_grad(d_grid, padded)
    up_term = jnp.einsum("brd,rh->bdh", normed, d_lifted, **f32).astype(jnp.bfloat16)
    norm_term = jnp.einsum("rh,bdh->brd", d_lifted, U, **f32).astype(jnp.bfloat16)
    branch, d_norm, g_up, g_down = scatter(branch_term, norm_term, up_term, down_term)
    own = tok.astype(jnp.float32)
    mixed = (own + branch).astype(jnp.bfloat16).reshape(tokens.shape)
    inv_own = lax.dynamic_slice_in_dim(inverse, zl * 256, 256, 0)
    hat = own * inv_own
    d_hat = d_norm * gain
    row_total = lax.psum(jnp.sum(d_hat * hat, axis=1), "fsdp")[:, None]
    grad_tokens = (
        (gout.astype(jnp.float32) + inv_own * (d_hat - hat * row_total / 4096.0))
        .astype(jnp.bfloat16)
        .reshape(tokens.shape)
    )
    wide = lax.dynamic_update_slice_in_dim(jnp.zeros((27, 1024), jnp.float32), conv_term, zl * B, 1)
    grad_conv, grad_gain = lax.psum((wide, jnp.sum(d_norm * hat, axis=0)), ("dp", "seq"))
    grad_up = g_up.transpose(1, 0, 2).reshape(512, 1024)
    grad_down = g_down.reshape(1024, 512)
    return (mixed, grad_tokens, grad_up, grad_down, grad_conv, grad_gain)


def solution(mesh):
    rows = P("dp", "seq", None, None, "fsdp")
    return jax.shard_map(
        per_device,
        mesh=mesh,
        in_specs=(rows, rows, P("fsdp"), P("seq", "fsdp"), P("fsdp", "seq"), P(None, "fsdp")),
        out_specs=(rows, rows, P("seq", "fsdp"), P("fsdp", "seq"), P(None, "fsdp"), P("fsdp")),
        check_vma=False,
    )
```

time: 697 us -> 334 us (0.48)
  waiting for transfers between devices: 484 us -> 8.9 us
  Pallas kernels: 0 us -> 194 us
  blocking collectives: 87.4 us -> 49.1 us
  matrix products: 39.5 us -> 23.3 us
  local copies, waits for them, and re-layouts: 32.6 us -> 17.7 us
  other arithmetic: 28.4 us -> 17.1 us
    all_gather x6 -> x0, waiting for transfers between devices: 233 us -> none  [the longest x1 107 us: per_device(): lax.all_gather(up_weight, 'seq', axis=0, tiled=True)]
    pallas_call x0 -> x2, Pallas kernels: none -> 194 us  [the longest x1 110 us: scatter(): pl.pallas_call(scatter_kernel, out_shape=[f32, f32, pair, pair], in_specs...]
    reduce_scatter x3 -> x0, waiting for transfers between devices: 181 us -> none  [the longest x1 106 us: per_device(): lax.psum_scatter(up_order.astype(jnp.bfloat16), ('dp', 'seq'), scatter_di...]
    psum x1, waiting for transfers between devices: 62.7 us -> 0.01 us  [per_device(): lax.psum((wide, jnp.sum(d_norm * hat, axis=0)), ('dp', 'seq'))]
    psum x1 -> x2, blocking collectives: 75.4 us -> 49.1 us  [the longest x1 36.7 us: per_device(): lax.psum((wide, jnp.sum(d_norm * hat, axis=0)), ('dp', 'seq'))]
    dot_general x6, matrix products: 39.5 us -> 23.3 us  [the longest x1 4.54 us: per_device(): jnp.einsum('brd,rh->bdh', normed, d_lifted, **f32).astype(jnp.bfloat16)]
    convert_element_type x2 -> x0, local copies, waits for them, and re-layouts: 16 us -> none  [the longest x1 8.02 us: per_device(): up_order.astype(jnp.bfloat16)]
    all_gather x1 -> x0, blocking collectives: 12 us -> none  [per_device(): lax.all_gather(gain.astype(jnp.bfloat16), 'fsdp', axis=0, tiled=True)]
  transfers between devices with their start and end apart: 14 -> 5, of which waited for: 10 -> 2; matrix products, arithmetic and copies ran while one was open for 14% -> 7% of each run, Pallas kernels for 0% -> 33%
where the time goes in v1:
time: 334 us; the launch traced here: 333 us
  Pallas kernels  194 us (58%)
  blocking collectives  49.1 us (15%)
  matrix products  23.3 us (7%)
  local copies, waits for them, and re-layouts  17.7 us (5%)
  other arithmetic  17.1 us (5%)
  between operations  14.4 us (4%)
  waiting for transfers between devices  8.9 us (3%)
  starting transfers between devices  8.74 us (3%)
    pallas_call x1, Pallas kernels, scatter(): pl.pallas_call(scatter_kernel, out_shape=[f32, f32, pair, pair], in_specs...  110 us
    pallas_call x1, Pallas kernels, gather(): pl.pallas_call(gather_kernel, out_shape=[blocks, blocks, blocks, blocks,...  84.1 us
    psum x1, blocking collectives, per_device(): lax.psum((wide, jnp.sum(d_norm * hat, axis=0)), ('dp', 'seq'))  36.7 us
    unnamed x38, local copies, waits for them, and re-layouts  12.8 us
    psum x1, blocking collectives, per_device(): row_total = lax.psum(jnp.sum(d_hat * hat, axis=1), 'fsdp')[:, None]  12.4 us
    ppermute x2, waiting for transfers between devices, with_halo(): high = lax.ppermute(block[:, 0:1], 'seq', backward)  8.88 us
  transfers between devices with their start and end apart: 5, of which 2 were waited for; matrix products, arithmetic and copies ran while one was open for 7% of the time, Pallas kernels for 33%

profile of v1, /device:TPU:0, one launch (start us, length us, event | category | flops | bytes accessed | tf_op | source)
XLA Modules:
  0.0 333.0 jit_solution(5919110990081029002)
XLA Ops:
  7.2 0.0 all-reduce.4.cloned.1.call-start
  7.2 0.7 broadcast_in_dim.4.gain
  7.9 0.0 copy-start.2
  7.9 0.9 copy-done.2
  8.8 1.2 copy-done.4
  10.1 1.2 copy-done.5
  11.3 0.9 copy-done.6
  12.2 84.1 %gather.1 = (bf16[8,512,512]{2,1,0:T(8,128)(2,1)S(1)}, bf16[8,512,512]{2,1,0:T(8,128)(2,1)S(1)}, bf16[8,512,512]{2,1,0:T(8,128)(2,1)S(1)}, bf16[8,512,512]{2,1,0:T(8,128)(2,1)S(1)}, f32[8,8,512]{2,1,0:T(8,128)S(1)}) custom-call(bf16[256,512]{1,0:T(8,128)(2,1)S(1)} %bitcast.130, bf16[256,512]{1,0:T(8,128)(2,1)S(1)} %bitcast.131, ...), custom_call_target="tpu_custom_call" | custom-call | tf_op jit(solution)/shard_map/gather/pallas_call | solution.py:221
  96.4 0.0 copy-start.10
  96.4 1.9 copy-done.10
  98.3 2.0 copy-done.12
  100.3 0.9 fusion
  101.2 2.4 fusion.8
  103.6 0.0 copy-done
  103.6 0.0 copy-done.8
  103.7 3.2 collective-permute-start
  106.9 1.5 collective-permute-start.1
  108.4 1.1 fusion.98
  109.5 0.1 dynamic-slice.3
  109.5 1.3 constant_dynamic-slice_fusion
  110.9 0.0 collective-permute-done
  110.9 2.8 collective-permute-done.1
  113.7 0.7 select_maximum_fusion.2
  114.5 0.0 copy-start.11
  114.5 4.3 %fusion.42 = (f32[2,4,8,8,512]{4,3,2,1,0:T(8,128)S(1)}, f32[2,4,8,8,512]{4,3,2,1,0:T(8,128)S(1)}) fusion(bf16[2,6,10,10,512]{4,3,2,1,0:T(8,128)(2,1)S(1)} %select_maximum_fusion.2, f32[512]{0:T(512)S(1)} %bitcast.165, f32[512]{0:T(512)S(1)} %bitcast.169, f32[512]{0:T(512)S(1)} %bitcast.171, f32[512]{0:T(512)S(1)} %bitcast.173, ...), kind=kLoop, calls=%fused_computation.111 | loop fusion | flops 25952256 | bytes 15521792 | tf_op jit(solution)/shard_map/add | solution.py:412
  118.8 0.3 multiply_convert_fusion
  119.1 0.0 copy-done.11
  119.2 0.0 copy-start.13
  119.2 4.5 %convert_bitcast_fusion.g_down = bf16[8,512,512]{2,1,0:T(8,128)(2,1)} fusion(bf16[8,512,512]{2,1,0:T(8,128)(2,1)S(1)} %copy-done.11, bf16[512,512,1]{1,0,2:T(8,128)(2,1)S(1)} %bitcast.145), kind=kOutput, calls=%fused_computation.36 | convolution fusion | flops 2149580800 | bytes 8912896 | tf_op jit(solution)/shard_map/rh,brd->bhd/dot_general | solution.py:461
  123.6 0.0 copy-done.13
  123.6 4.3 %convert_bitcast_fusion.2.branch = bf16[8,512,512]{2,1,0:T(8,128)(2,1)} fusion(bf16[512,512,1]{1,0,2:T(8,128)(2,1)S(1)} %bitcast.146, bf16[8,512,512]{2,1,0:T(8,128)(2,1)S(1)} %copy-done.13), kind=kOutput, calls=%fused_computation.38 | convolution fusion | flops 2149580800 | bytes 8912896 | tf_op jit(solution)/shard_map/rh,bhd->brd/dot_general | solution.py:459
  128.0 3.2 fusion.78
  131.2 2.6 fusion.82
  133.9 2.5 collective-permute-start.2
  136.4 1.5 collective-permute-start.3
  137.9 0.2 multiply_reduce_fusion
  138.1 0.1 stack.111
  138.3 0.0 copy-start.15
  138.3 0.6 copy-done.15
  139.0 0.0 all-reduce.4.cloned.1.call-update
  139.0 0.0 collective-permute-done.2
  139.0 6.0 %collective-permute-done.3 = bf16[2,1,8,8,512]{4,3,2,1,0:T(8,128)(2,1)S(1)} collective-permute-done((bf16[2,1,8,8,512]{4,3,2,1,0:T(8,128)(2,1)S(1)}, bf16[2,1,8,8,512]{4,3,2,1,0:T(8,128)(2,1)S(1)}, u32[]{:S(2)}, u32[]{:S(2)}) %collective-permute-start.3) | collective-permute-done | bytes 131104 | tf_op jit(solution)/shard_map/ppermute | solution.py:404
  145.0 0.7 select_maximum_fusion
  145.8 0.0 copy-start.1
  145.8 3.7 %fusion.83 = bf16[2,4,8,8,512]{4,3,2,1,0:T(8,128)(2,1)S(1)} fusion(bf16[2,4,8,8,512]{4,3,2,1,0:T(8,128)(2,1)S(1)} %bitcast.134, bf16[2,6,10,10,512]{4,3,2,1,0:T(8,128)(2,1)S(1)} %select_maximum_fusion, bf16[2,1,8,8,512]{4,3,2,1,0:T(8,128)(2,1)S(1)} %collective-permute-done.3, bf16[2,1,8,8,512]{4,3,2,1,0:T(8,128)(2,1)S(1)} %collective-permute-done.2, ...), kind=kLoop, calls=%fused_computation.154 | loop fusion | flops 21757952 | bytes 13948928 | tf_op jit(solution)/shard_map/convert_element_type | solution.py:465
  149.5 0.0 copy-done.1
  149.5 0.0 copy-start.9
  149.5 4.5 %convolution_convert_fusion.g_up = bf16[8,512,512]{2,1,0:T(8,128)(2,1)} fusion(bf16[512,512,1]{1,0,2:T(8,128)(2,1)S(1)} %bitcast.143, bf16[8,512,512]{2,1,0:T(8,128)(2,1)S(1)} %copy-done.1, f32[8,512]{1,0:T(8,128)S(1)} %bitcast.204, f32[512]{0:T(512)S(1)} %add_rsqrt_fusion), kind=kOutput, calls=%fused_computation.42 | convolution fusion | flops 2157969408 | bytes 8931328 | tf_op jit(solution)/shard_map/brd,rh->bdh/dot_general | solution.py:467
  154.0 0.0 copy-done.9
  154.0 4.3 %convert_bitcast_fusion.1.norm = bf16[8,512,512]{2,1,0:T(8,128)(2,1)} fusion(bf16[8,512,512]{2,1,0:T(8,128)(2,1)S(1)} %copy-done.9, bf16[512,512,1]{1,0,2:T(8,128)(2,1)S(1)} %bitcast.144), kind=kOutput, calls=%fused_computation.37 | convolution fusion | flops 2149580800 | bytes 8912896 | tf_op jit(solution)/shard_map/rh,bdh->brd/dot_general | solution.py:468
  158.4 109.6 %scatter.1 = (f32[256,512]{1,0:T(8,128)}, f32[256,512]{1,0:T(8,128)}, bf16[2,512,512]{2,1,0:T(8,128)(2,1)}, bf16[2,512,512]{2,1,0:T(8,128)(2,1)}) custom-call(bf16[8,512,512]{2,1,0:T(8,128)(2,1)} %convert_bitcast_fusion.2.branch, bf16[8,512,512]{2,1,0:T(8,128)(2,1)} %convert_bitcast_fusion.1.norm, bf16[8,512,512]{2,1,0:T(8,128)(2,1)} %convolution_convert_fusion.g_up, ...), custom_call_target="tpu_custom_call" | custom-call | tf_op jit(solution)/shard_map/scatter/pallas_call | solution.py:386
  268.0 0.0 copy-start.14
  268.0 0.0 copy-done.3
  268.0 0.0 copy-done.16
  268.0 1.4 fusion.93
  269.4 12.4 %psum.21 = f32[256]{0:T(256)S(1)} all-reduce(f32[256]{0:T(256)S(1)} %get-tuple-element.57), channel_id=1, replica_groups=mesh['dp'=2,'fsdp'=8,'seq'=8] {'fsdp'}, use_global_device_ids=true, to_apply=%region_2.3 | all-reduce | flops 256 | bytes 2048 | tf_op jit(solution)/shard_map/psum | solution.py:475
  281.8 0.0 copy-done.7
  281.8 2.2 fusion.92
  284.0 1.5 copy.24
  285.5 1.3 copy.25
  286.8 36.7 %psum.23 = f32[512]{0:T(512)} all-reduce(f32[512]{0:T(512)S(1)} %get-tuple-element.56), channel_id=1, replica_groups=mesh['dp'=2,'fsdp'=8,'seq'=8] {'dp','seq'}, use_global_device_ids=true, to_apply=%region_32.33 | all-reduce | flops 512 | bytes 4096 | tf_op jit(solution)/shard_map/psum | solution.py:482
  323.6 0.0 copy-done.14
  323.6 1.0 copy.38
  324.5 1.6 copy.39
  (17 shorter events, 0.1 us)
Async XLA Ops:
  7.2 316.4 %all-reduce.4.cloned.1.call-start = ((), (), s32[]{:S(2)}) async-start(), calls=%async_computation | async-start | bytes 262144 | tf_op jit(solution)/shard_map/psum | solution.py:482
  7.9 0.9 copy-start.2
  8.8 1.2 copy-start.4
  10.1 1.2 copy-start.5
  11.3 0.9 copy-start.6
  96.4 1.9 copy-start.10
  98.3 2.0 copy-start.12
  100.3 3.3 copy-start
  100.3 3.3 copy-start.8
  103.7 7.2 %collective-permute-start = (bf16[2,1,8,8,512]{4,3,2,1,0:T(8,128)(2,1)S(1)}, bf16[2,1,8,8,512]{4,3,2,1,0:T(8,128)(2,1)S(1)}, u32[]{:S(2)}, u32[]{:S(2)}) collective-permute-start(bf16[2,1,8,8,512]{4,3,2,1,0:T(8,128)(2,1)S(1)} %get-tuple-element.68), channel_id=1, source_target_pairs={{0,1},{1,2},{2,3},{3,4},{4,5},{5,6},{6,7},{8,9},{9,10},{10,11},{11... | collective-permute-start | bytes 393224 | tf_op jit(solution)/shard_map/ppermute | solution.py:403
  106.9 6.9 %collective-permute-start.1 = (bf16[2,1,8,8,512]{4,3,2,1,0:T(8,128)(2,1)S(1)}, bf16[2,1,8,8,512]{4,3,2,1,0:T(8,128)(2,1)S(1)}, u32[]{:S(2)}, u32[]{:S(2)}) collective-permute-start(bf16[2,1,8,8,512]{4,3,2,1,0:T(8,128)(2,1)S(1)} %get-tuple-element.69), channel_id=1, source_target_pairs={{1,0},{2,1},{3,2},{4,3},{5,4},{6,5},{7,6},{9,8},{10,9},{11,10},{12... | collective-permute-start | bytes 393224 | tf_op jit(solution)/shard_map/ppermute | solution.py:404
  114.5 4.7 %copy-start.11 = (bf16[8,512,512]{2,1,0:T(8,128)(2,1)S(1)}, bf16[8,512,512]{2,1,0:T(8,128)(2,1)}, u32[]{:S(2)}) copy-start(bf16[8,512,512]{2,1,0:T(8,128)(2,1)} %copy-done.10) | copy-start | bytes 12582916
  119.2 4.5 %copy-start.13 = (bf16[8,512,512]{2,1,0:T(8,128)(2,1)S(1)}, bf16[8,512,512]{2,1,0:T(8,128)(2,1)}, u32[]{:S(2)}) copy-start(bf16[8,512,512]{2,1,0:T(8,128)(2,1)} %copy-done.12) | copy-start | bytes 12582916
  133.9 5.1 %collective-permute-start.2 = (bf16[2,1,8,8,512]{4,3,2,1,0:T(8,128)(2,1)S(1)}, bf16[2,1,8,8,512]{4,3,2,1,0:T(8,128)(2,1)S(1)}, u32[]{:S(2)}, u32[]{:S(2)}) collective-permute-start(bf16[2,1,8,8,512]{4,3,2,1,0:T(8,128)(2,1)S(1)} %get-tuple-element.66), channel_id=1, source_target_pairs={{0,1},{1,2},{2,3},{3,4},{4,5},{5,6},{6,7},{8,9},{9,10},{10,11},{11... | collective-permute-start | bytes 393224 | tf_op jit(solution)/shard_map/ppermute | solution.py:403
  136.4 8.6 %collective-permute-start.3 = (bf16[2,1,8,8,512]{4,3,2,1,0:T(8,128)(2,1)S(1)}, bf16[2,1,8,8,512]{4,3,2,1,0:T(8,128)(2,1)S(1)}, u32[]{:S(2)}, u32[]{:S(2)}) collective-permute-start(bf16[2,1,8,8,512]{4,3,2,1,0:T(8,128)(2,1)S(1)} %get-tuple-element.67), channel_id=1, source_target_pairs={{1,0},{2,1},{3,2},{4,3},{5,4},{6,5},{7,6},{9,8},{10,9},{11,10},{12... | collective-permute-start | bytes 393224 | tf_op jit(solution)/shard_map/ppermute | solution.py:404
  138.3 0.7 copy-start.15
  145.8 3.7 %copy-start.1 = (bf16[8,512,512]{2,1,0:T(8,128)(2,1)S(1)}, bf16[8,512,512]{2,1,0:T(8,128)(2,1)}, u32[]{:S(2)}) copy-start(bf16[8,512,512]{2,1,0:T(8,128)(2,1)} %copy-done) | copy-start | bytes 12582916
  149.5 4.6 %copy-start.9 = (bf16[8,512,512]{2,1,0:T(8,128)(2,1)S(1)}, bf16[8,512,512]{2,1,0:T(8,128)(2,1)}, u32[]{:S(2)}) copy-start(bf16[8,512,512]{2,1,0:T(8,128)(2,1)} %copy-done.8) | copy-start | bytes 12582916
  158.4 109.6 %copy-start.3 = (bf16[1,4,8,8,512]{4,3,2,1,0:T(8,128)(2,1)S(1)}, bf16[1,4,8,8,512]{4,3,2,1,0:T(8,128)(2,1)}, u32[]{:S(2)}) copy-start(bf16[1,4,8,8,512]{4,3,2,1,0:T(8,128)(2,1)} %param.6) | copy-start | bytes 786436
  158.4 109.6 %copy-start.16 = (f32[512]{0:T(512)S(1)}, f32[512]{0:T(512)}, u32[]{:S(2)}) copy-start(f32[512]{0:T(512)} %param.8) | copy-start | bytes 6148
  158.4 123.4 %copy-start.7 = (bf16[1,4,8,8,512]{4,3,2,1,0:T(8,128)(2,1)S(1)}, bf16[1,4,8,8,512]{4,3,2,1,0:T(8,128)(2,1)}, u32[]{:S(2)}) copy-start(bf16[1,4,8,8,512]{4,3,2,1,0:T(8,128)(2,1)} %param.7) | copy-start | bytes 786436
  268.0 55.6 %copy-start.14 = (bf16[2,512,512]{2,1,0:T(8,128)(2,1)S(1)}, bf16[2,512,512]{2,1,0:T(8,128)(2,1)}, u32[]{:S(2)}) copy-start(bf16[2,512,512]{2,1,0:T(8,128)(2,1)} %get-tuple-element.23) | copy-start | bytes 3145732
Sparse Core Ops, SparseCore 0:
  139.1 89.3 all-reduce.3

commit v2 on v1

v2 whole, which is shorter than its diff:
```python
import jax
import jax.numpy as jnp
from jax import lax
from jax.experimental import pallas as pl
from jax.experimental.pallas import tpu as pltpu
from jax.sharding import PartitionSpec as P

MESH = pl.DeviceIdType.MESH
gelu_scale = 0.7978845608028654
gelu_cubic = 0.044715
epsilon = 1e-06
B = 512


class Place:
    def __init__(self):
        self.zl = lax.axis_index("dp")
        self.f = lax.axis_index("fsdp")
        self.s = lax.axis_index("seq")
        self.x, self.c = lax.div(self.f, 2), lax.rem(self.f, 2)
        self.zh, self.y = lax.div(self.s, 4), lax.rem(self.s, 4)
        self.xs = [lax.rem(self.x + k, 4) for k in range(4)]
        self.ys = [lax.rem(self.y + k, 4) for k in range(4)]
        self.other_zl = {"dp": 1 - self.zl}
        self.other_core = {"fsdp": self.feat(0, 1)}
        self.x_up, self.x_down = {"fsdp": self.feat(1)}, {"fsdp": self.feat(3)}
        self.other_zh = {"seq": self.slab(0, 1)}
        self.y_up, self.y_down = {"seq": self.slab(1)}, {"seq": self.slab(3)}

    def feat(self, k, flip=0):
        return self.xs[k] * 2 + (1 - self.c if flip else self.c)

    def slab(self, k, flip=0):
        return (1 - self.zh if flip else self.zh) * 4 + self.ys[k]

    def partners(self):
        return [self.other_zl, self.other_core, self.x_up, self.x_down, self.other_zh, self.y_up, self.y_down]


class Wires:
    def __init__(self, send, recv):
        self.send, self.recv, self.copies, self.left = send, recv, [], 0

    def start(self, src, dst, where):
        i = len(self.copies)
        copy = pltpu.make_async_remote_copy(
            src_ref=src, dst_ref=dst, send_sem=self.send.at[i], recv_sem=self.recv.at[i],
            device_id=where, device_id_type=MESH,
        )
        copy.start()
        self.copies.append(copy)
        return copy

    def flush(self, until=None):
        for copy in self.copies[self.left : until]:
            copy.wait_send()
        self.left = len(self.copies) if until is None else until


def meet(partners):
    barrier = pltpu.get_barrier_semaphore()
    for where in partners:
        pl.semaphore_signal(barrier, inc=1, device_id=where, device_id_type=MESH)
    pl.semaphore_wait(barrier, len(partners))


class WeightGather:
    def __init__(self, me, wires, own, buf):
        self.me, self.wires, self.own, self.buf = me, wires, own, buf

    def start_z(self):
        self.z = self.wires.start(self.own, self.buf.at[self.me.s], self.me.other_zh)

    def start_y(self):
        self.up = self.wires.start(self.own, self.buf.at[self.me.s], self.me.y_up)
        self.down = self.wires.start(self.own, self.buf.at[self.me.s], self.me.y_down)

    def forward(self, flip):
        me, buf = self.me, self.buf
        below, above = me.slab(3, flip), me.slab(1, flip)
        self.up.wait_recv()
        part = buf.at[below, pl.ds(0, B // 2)]
        first = self.wires.start(part, part, me.y_up)
        self.down.wait_recv()
        part = buf.at[above, pl.ds(B // 2, B // 2)]
        return first, self.wires.start(part, part, me.y_down)

    def forward_own(self):
        self.far = self.forward(0)

    def start_other(self):
        self.z.wait_recv()
        block = self.buf.at[self.me.slab(0, 1)]
        self.up = self.wires.start(block, block, self.me.y_up)
        self.down = self.wires.start(block, block, self.me.y_down)

    def forward_other(self):
        self.far_other = self.forward(1)

    def wait_far(self):
        for copy in self.far:
            copy.wait_recv()

    def wait_far_other(self):
        for copy in self.far_other:
            copy.wait_recv()


class TokenGather:
    def __init__(self, me, wires, own, buf):
        self.me, self.wires, self.own, self.buf = me, wires, own, buf
        self.cores = []

    def rows(self, half, part=None):
        if part is None:
            return pl.ds(pl.multiple_of(half * 256, 256), 256)
        return pl.ds(pl.multiple_of(half * 256 + part * 128, 128), 128)

    def start_own(self):
        me = self.me
        dst = self.buf.at[me.f, self.rows(me.zl)]
        self.z = self.wires.start(self.own, dst, me.other_zl)
        self.ring = [self.wires.start(self.own, dst, where) for where in (me.x_up, me.x_down)]
        self.cores.append(self.wires.start(self.own, dst, me.other_core))

    def to_core(self, k, half):
        block = self.buf.at[self.me.feat(k), self.rows(half)]
        self.cores.append(self.wires.start(block, block, self.me.other_core))

    def forward(self, half):
        me, buf, ring = self.me, self.buf, self.ring
        ring[0].wait_recv()
        part = buf.at[me.feat(3), self.rows(half, 0)]
        first = self.wires.start(part, part, me.x_up)
        ring[1].wait_recv()
        part = buf.at[me.feat(1), self.rows(half, 1)]
        self.far = first, self.wires.start(part, part, me.x_down)
        self.to_core(3, half)
        self.to_core(1, half)

    def start_other(self):
        me = self.me
        self.z.wait_recv()
        block = self.buf.at[me.f, self.rows(1 - me.zl)]
        self.ring = [self.wires.start(block, block, where) for where in (me.x_up, me.x_down)]
        self.to_core(0, 1 - me.zl)

    def finish_half(self, half):
        for copy in self.far:
            copy.wait_recv()
        self.to_core(2, half)

    def wait_cores(self):
        for copy in self.cores:
            copy.wait_recv()


CHUNK = 64


def chunk(r, base=0):
    return pl.ds(pl.multiple_of(base + r * CHUNK, CHUNK), CHUNK)


def loop(count, body):
    def step(i, carry):
        body(i)
        return carry

    lax.fori_loop(0, count, step, 0)


def add_into(dst, *parts):
    def body(r):
        rows = chunk(r)
        total = parts[0][rows, :].astype(jnp.float32)
        for part in parts[1:]:
            total = total + part[rows, :].astype(jnp.float32)
        dst[rows, :] = total.astype(dst.dtype)

    loop(dst.shape[0] // CHUNK, body)


class RowScatter:
    def __init__(self, me, wires, terms, from_core, from_far, from_near, to_z, from_z):
        self.me, self.wires, self.terms = me, wires, terms
        self.from_core, self.from_far, self.from_near = from_core, from_far, from_near
        self.to_z, self.from_z = to_z, from_z

    def start_core(self):
        me = self.me
        self.core = {}
        for k in (2, 1, 3, 0):
            self.core[k] = self.wires.start(
                self.terms.at[me.feat(k, 1)], self.from_core.at[me.xs[k]], me.other_core
            )

    def held(self, k):
        return self.terms.at[self.me.feat(k)]

    def join(self, k):
        self.core[k].wait_recv()
        add_into(self.held(k), self.held(k), self.from_core.at[self.me.xs[k]])

    def start_far(self):
        me = self.me
        self.join(2)
        self.far = [
            self.wires.start(self.held(2).at[pl.ds(0, 256)], self.from_far.at[0], me.x_up),
            self.wires.start(self.held(2).at[pl.ds(256, 256)], self.from_far.at[1], me.x_down),
        ]
        self.join(1)
        self.join(3)
        self.join(0)

    def start_near(self):
        me = self.me
        self.far[0].wait_recv()
        part = self.held(1).at[pl.ds(0, 256)]
        add_into(part, part, self.from_far.at[0])
        first = self.wires.start(self.held(1), self.from_near.at[0], me.x_up)
        self.far[1].wait_recv()
        part = self.held(3).at[pl.ds(256, 256)]
        add_into(part, part, self.from_far.at[1])
        self.near = first, self.wires.start(self.held(3), self.from_near.at[1], me.x_down)

    def half(self, zl):
        rows = pl.ds(pl.multiple_of(zl * 256, 256), 256)
        return [self.held(0).at[rows], self.from_near.at[0, rows], self.from_near.at[1, rows]]

    def start_z(self):
        me = self.me
        self.near[0].wait_recv()
        self.near[1].wait_recv()
        add_into(self.to_z, *self.half(1 - me.zl))
        self.z = self.wires.start(self.to_z, self.from_z, me.other_zl)

    def wait(self):
        self.z.wait_recv()
        self.parts = self.half(self.me.zl) + [self.from_z]

    def result(self, rows):
        total = self.parts[0][rows, :].astype(jnp.float32)
        for part in self.parts[1:]:
            total = total + part[rows, :].astype(jnp.float32)
        return total

    @staticmethod
    def scratch():
        blocks = lambda *shape: pltpu.VMEM(shape, jnp.bfloat16)
        return [blocks(4, B, B), blocks(2, 256, B), blocks(2, B, B), blocks(256, B), blocks(256, B)]


class WeightScatter:
    def __init__(self, me, wires, terms, from_far, from_near, to_z, from_z):
        self.me, self.wires, self.terms = me, wires, terms
        self.from_far, self.from_near, self.to_z, self.from_z = from_far, from_near, to_z, from_z

    def start_far(self):
        me, y = self.me, self.me.ys
        start = self.wires.start
        self.far = [
            start(self.terms.at[y[2]], self.from_far.at[0], me.y_up),
            start(self.terms.at[4 + y[2]], self.from_far.at[1], me.y_down),
        ]
        self.near = [
            start(self.terms.at[4 + y[1]], self.from_near.at[1], me.y_up),
            start(self.terms.at[y[3]], self.from_near.at[2], me.y_down),
        ]

    def start_near(self):
        me, y = self.me, self.me.ys
        start = self.wires.start
        self.far[0].wait_recv()
        block = self.terms.at[y[1]]
        add_into(block, block, self.from_far.at[0])
        self.near.append(start(block, self.from_near.at[0], me.y_up))
        self.far[1].wait_recv()
        block = self.terms.at[4 + y[3]]
        add_into(block, block, self.from_far.at[1])
        self.near.append(start(block, self.from_near.at[3], me.y_down))

    def parts(self, zh):
        return [self.terms.at[zh * 4 + self.me.y], self.from_near.at[zh], self.from_near.at[2 + zh]]

    def start_z(self):
        for copy in self.near:
            copy.wait_recv()
        add_into(self.to_z, *self.parts(1 - self.me.zh))
        self.z = self.wires.start(self.to_z, self.from_z, self.me.other_zh)

    def start_out(self, out, sem):
        self.z.wait_recv()
        block = self.terms.at[self.me.s]
        add_into(block, *self.parts(self.me.zh), self.from_z)
        self.last = self.wires.start(block, out, self.me.other_zl)
        self.here = pltpu.make_async_copy(block, out, sem)
        self.here.start()

    def wait_out(self):
        self.last.wait_recv()
        self.here.wait()

    @staticmethod
    def scratch():
        blocks = lambda *shape: pltpu.VMEM(shape, jnp.bfloat16)
        return [blocks(2, B, B), blocks(4, B, B), blocks(B, B), blocks(B, B)]


class Halo:
    def __init__(self, me, wires, planes, came, field):
        self.me, self.wires, self.planes, self.came, self.field = me, wires, planes, came, field

    def start(self):
        me = self.me
        above, below = {"seq": lax.rem(me.s + 1, 8)}, {"seq": lax.rem(me.s + 7, 8)}
        self.copies = [
            self.wires.start(self.planes.at[1], self.came.at[0], above),
            self.wires.start(self.planes.at[0], self.came.at[1], below),
        ]

    def wait(self):
        edges = [(me_s != edge).astype(jnp.float32) for me_s, edge in ((self.me.s, 0), (self.me.s, 7))]
        for copy in self.copies:
            copy.wait_recv()
        for side in range(2):
            for snap in range(2):
                plane = self.came[side, snap].astype(jnp.float32) * edges[side]
                self.field[snap * 6 + side * 5, 1:9] = plane.reshape(8, 8, B)


def spread(total, field, planes):
    def body(i):
        snap, p = lax.div(i, 4), lax.rem(i, 4)
        rounded = total[chunk(i), :].astype(jnp.bfloat16)
        field[snap * 6 + 1 + p, 1:9] = rounded.astype(jnp.float32).reshape(8, 8, B)

    loop(8, body)
    for side in range(2):
        for snap in range(2):
            planes[side, snap] = total[pl.ds(snap * 256 + side * 192, 64), :].astype(jnp.bfloat16)


def shift(value, by):
    cells = lax.broadcasted_iota(jnp.int32, value.shape, 1)
    moved = pltpu.roll(value, by % 8, 1)
    return jnp.where(cells == (0 if by == 1 else 7), 0.0, moved)


def conv_planes(field, taps, flipped, count, which, finish):
    def body(i):
        snap, p = which(i)
        for lane in range(0, B, 128):
            lanes = pl.ds(lane, 128)
            by_c = [None] * 3
            for a in range(3):
                for b in range(3):
                    window = field[snap * 6 + p + a, pl.ds(b, 8), :, lanes]
                    for c in range(3):
                        index = a * 9 + b * 3 + c
                        index = 26 - index if flipped else index
                        term = window * taps[pl.ds(index, 1), lanes].reshape(1, 1, 128)
                        by_c[c] = term if by_c[c] is None else by_c[c] + term
            total = by_c[1] + shift(by_c[0], 1) + shift(by_c[2], -1)
            finish(chunk(snap * 4 + p), lanes, total.reshape(CHUNK, 128))

    loop(count, body)


def inner(i):
    return lax.div(i, 2), 1 + lax.rem(i, 2)


def outer(i):
    return lax.div(i, 2), 3 * lax.rem(i, 2)


def gelu_pair(preact):
    inner_value = gelu_scale * (preact + gelu_cubic * preact * preact * preact)
    tangent = jnp.tanh(inner_value)
    value = 0.5 * preact * (1.0 + tangent)
    slope = 0.5 * (1.0 + tangent) + 0.5 * preact * (1.0 - tangent * tangent) * gelu_scale * (
        1.0 + 3.0 * gelu_cubic * preact * preact
    )
    return (value, slope)


def dot(left, right, left_dim, right_dim):
    return lax.dot_general(
        left, right, (((left_dim,), (right_dim,)), ((), ())), preferred_element_type=jnp.float32
    )


def block_kernel(
    tok, gout, gain, up, down, taps_all,
    mixed_out, tokens_out, up_out, down_out, conv_out, gain_out,
    T, G, U, D, N, PB, GD, gains, taps, field, d_field, total, slope, active, d_lifted, inverse,
    planes, came, d_norm, row_part, conv_sums, conv_terms, row_terms, gain_terms,
    b0, b1, b2, b3, b4, n0, n1, n2, n3, n4, w0, w1, w2, w3, v0, v1, v2, v3,
    local, send, recv,
):
    me = Place()
    group = me.zl * 8 + me.s
    peers = [lax.rem(me.f + k, 8) for k in range(1, 8)]
    slabs = [lax.rem(me.s + k, 8) for k in range(1, 8)]
    groups = [lax.rem(group + k, 16) for k in range(1, 16)]
    groups = [(k, {"dp": lax.div(k, 8), "seq": lax.rem(k, 8)}) for k in groups]
    meet([{"fsdp": p} for p in peers] + [where for _, where in groups])
    wires = Wires(send, recv)
    hidden = pl.ds(pl.multiple_of(me.zl * B, B), B)
    up_own, down_own = up.at[:, hidden], down.at[hidden, :]
    u, d = WeightGather(me, wires, up_own, U), WeightGather(me, wires, down_own, D)
    t, g = TokenGather(me, wires, tok, T), TokenGather(me, wires, gout, G)
    PN, GU = T, D
    b = RowScatter(me, wires, PB, b0, b1, b2, b3, b4)
    n = RowScatter(me, wires, PN, n0, n1, n2, n3, n4)
    gd = WeightScatter(me, wires, GD, w0, w1, w2, w3)
    gu = WeightScatter(me, wires, GU, v0, v1, v2, v3)

    u.start_z()
    u.start_y()
    t.start_own()
    gain_copies = [wires.start(gain, gains.at[me.f], {"fsdp": p}) for p in peers]
    own = t.rows(me.zl)
    here = [
        pltpu.make_async_copy(src, dst, local.at[i])
        for i, (src, dst) in enumerate(
            [
                (tok, T.at[me.f, own]),
                (gain, gains.at[me.f]),
                (up_own, U.at[me.s]),
                (taps_all.at[:, hidden], taps),
                (gout, G.at[me.f, own]),
                (down_own, D.at[me.s]),
            ]
        )
    ]
    for copy in here:
        copy.start()
    field[...] = jnp.zeros_like(field)
    d_field[...] = jnp.zeros_like(d_field)
    t.forward(me.zl)
    t.start_other()
    d.start_z()
    g.start_own()
    u.forward_own()
    u.start_other()
    d.start_y()
    t.finish_half(me.zl)
    t.forward(1 - me.zl)
    t.finish_half(1 - me.zl)
    for copy in here:
        copy.wait()
    for copy in gain_copies:
        copy.wait_recv()
    g.forward(me.zl)
    g.start_other()
    t.wait_cores()

    def normalise(r):
        rows = chunk(r)
        squares = jnp.zeros((CHUNK, 128), jnp.float32)
        for k in range(8):
            for lane in range(0, B, 128):
                value = T[k, rows, pl.ds(lane, 128)].astype(jnp.float32)
                squares = squares + value * value
        mean = jnp.sum(squares, axis=1, keepdims=True) / 4096.0
        inv = jnp.broadcast_to(lax.rsqrt(mean + epsilon), (CHUNK, 128))
        inverse[rows, :] = inv
        for k in range(8):
            for lane in range(0, B, 128):
                lanes = pl.ds(lane, 128)
                value = T[k, rows, lanes].astype(jnp.float32) * inv * gains[k, 0:1, lanes]
                N[k, rows, lanes] = value.astype(jnp.bfloat16)

    loop(8, normalise)
    total[...] = jnp.zeros_like(total)

    def lift(zh):
        def body(i):
            j = zh * 4 + i
            total[...] += dot(N[j], U[j], 1, 0)

        loop(4, body)

    u.wait_far()
    u.forward_other()
    lift(me.zh)
    d.forward_own()
    d.start_other()
    g.finish_half(me.zl)
    g.forward(1 - me.zl)
    u.wait_far_other()
    lift(1 - me.zh)
    spread(total, field, planes.at[0])
    halo = Halo(me, wires, planes.at[0], came.at[0], field)
    halo.start()

    def activate(rows, lanes, preact):
        value, rate = gelu_pair(preact)
        active[rows, lanes] = value.astype(jnp.bfloat16)
        slope[rows, lanes] = rate

    conv_planes(field, taps, False, 4, inner, activate)
    g.finish_half(1 - me.zl)
    halo.wait()
    conv_planes(field, taps, False, 4, outer, activate)
    g.wait_cores()

    def down_term(j):
        GD[j] = dot(active[...], G[j], 0, 0).astype(jnp.bfloat16)

    loop(8, down_term)
    d.wait_far()
    d.forward_other()
    gathered = len(wires.copies)
    gd.start_far()
    total[...] = jnp.zeros_like(total)

    def d_active(zh):
        def body(i):
            j = zh * 4 + i
            total[...] += dot(G[j], D[j], 1, 1)

        loop(4, body)

    d_active(me.zh)
    d.wait_far_other()
    d_active(1 - me.zh)

    def d_preact(r):
        total[chunk(r), :] = total[chunk(r), :] * slope[chunk(r), :]

    loop(8, d_preact)
    spread(total, d_field, planes.at[1])
    d_halo = Halo(me, wires, planes.at[1], came.at[1], d_field)
    d_halo.start()

    def branch_term(j):
        PB[j] = dot(active[...], D[j], 1, 0).astype(jnp.bfloat16)

    loop(8, branch_term)
    b.start_core()

    def d_lift(rows, lanes, value):
        d_lifted[rows, lanes] = value.astype(jnp.bfloat16)

    conv_planes(d_field, taps, True, 4, inner, d_lift)
    d_halo.wait()
    conv_planes(d_field, taps, True, 4, outer, d_lift)
    b.start_far()
    gd.start_near()
    wires.flush(gathered)

    def up_term(j):
        GU[j] = dot(N[j], d_lifted[...], 0, 0).astype(jnp.bfloat16)

    loop(8, up_term)
    gu.start_far()

    def norm_term(j):
        PN[j] = dot(d_lifted[...], U[j], 1, 1).astype(jnp.bfloat16)

    loop(8, norm_term)
    n.start_core()
    b.start_near()
    n.start_far()
    gd.start_z()

    conv_sums[...] = jnp.zeros_like(conv_sums)

    def taps_grad(i):
        snap, p = lax.div(i, 4), lax.rem(i, 4)
        for lane in range(0, B, 128):
            lanes = pl.ds(lane, 128)
            here_d = d_field[snap * 6 + 1 + p, pl.ds(1, 8), :, lanes]
            by_c = [shift(here_d, -1), here_d, shift(here_d, 1)]
            for a in range(3):
                for b_ in range(3):
                    window = field[snap * 6 + p + a, pl.ds(b_, 8), :, lanes]
                    for c in range(3):
                        term = jnp.sum(by_c[c] * window, axis=0)
                        conv_sums[a * 9 + b_ * 3 + c, :, lanes] += term

    loop(8, taps_grad)
    conv_terms[me.s] = jnp.sum(conv_sums[...], axis=1).astype(jnp.bfloat16)
    conv_copies = [wires.start(conv_terms.at[me.s], conv_terms.at[me.s], {"seq": k}) for k in slabs]

    b.start_z()
    n.start_near()
    gd.start_out(down_out.at[hidden, :], local.at[0])
    gu.start_near()
    b.wait()

    def mix(r):
        rows = chunk(r)
        mixed_out[rows, :] = (tok[rows, :].astype(jnp.float32) + b.result(rows)).astype(jnp.bfloat16)

    loop(4, mix)
    for copy in conv_copies:
        copy.wait_recv()
    conv = conv_terms[0].astype(jnp.float32)
    for k in range(1, 8):
        conv = conv + conv_terms[k].astype(jnp.float32)
    conv_out[me.zl] = conv
    conv_copy = wires.start(conv_out.at[me.zl], conv_out.at[me.zl], me.other_zl)
    n.start_z()
    n.wait()

    def rows_part(r, gain_sum):
        rows = chunk(r)
        whole = n.result(rows)
        d_norm[rows, :] = whole
        inv = inverse[chunk(r, me.zl * 256), :]
        part = jnp.zeros((CHUNK, 128), jnp.float32)
        sums = []
        for lane in range(0, B, 128):
            lanes = slice(lane, lane + 128)
            with_hat = whole[:, lanes] * (tok[rows, lanes].astype(jnp.float32) * inv)
            part = part + with_hat * gain[0:1, lanes]
            sums.append(jnp.sum(with_hat.reshape(8, 8, 128), axis=0))
        row_part[rows, :] = part
        return gain_sum + jnp.concatenate(sums, axis=1)

    gain_sum = lax.fori_loop(0, 4, rows_part, jnp.zeros((8, B), jnp.float32))
    row_sum = jnp.sum(jnp.transpose(row_part[...]), axis=0, keepdims=True)
    row_terms[me.f] = jnp.broadcast_to(row_sum, (8, 256))
    row_copies = [wires.start(row_terms.at[me.f], row_terms.at[me.f], {"fsdp": p}) for p in peers]
    gain_terms[group] = jnp.broadcast_to(jnp.sum(gain_sum, axis=0, keepdims=True), (8, B))
    last_copies = [wires.start(gain_terms.at[group], gain_terms.at[group], where) for _, where in groups]

    gu.start_z()
    for copy in row_copies:
        copy.wait_recv()
    rows_sum = row_terms[0]
    for k in range(1, 8):
        rows_sum = rows_sum + row_terms[k]
    row_part[...] = jnp.transpose(jnp.broadcast_to(rows_sum[0:1, :], (128, 256)))

    def finish(r):
        rows = chunk(r)
        inv = inverse[chunk(r, me.zl * 256), :]
        share = row_part[rows, :] / 4096.0
        for lane in range(0, B, 128):
            lanes = slice(lane, lane + 128)
            hat = tok[rows, lanes].astype(jnp.float32) * inv
            value = inv * (d_norm[rows, lanes] * gain[0:1, lanes] - hat * share)
            tokens_out[rows, lanes] = (gout[rows, lanes].astype(jnp.float32) + value).astype(jnp.bfloat16)

    loop(4, finish)
    gu.start_out(up_out.at[:, hidden], local.at[1])
    for copy in last_copies:
        copy.wait_recv()
    all_gain = gain_terms[0]
    for k in range(1, 16):
        all_gain = all_gain + gain_terms[k]
    gain_out[...] = all_gain
    conv_copy.wait_recv()
    gd.wait_out()
    gu.wait_out()
    wires.flush()


def block(tok, gout, gain, up, down, taps):
    vmem = pl.BlockSpec(memory_space=pltpu.VMEM)
    anywhere = pl.BlockSpec(memory_space=pl.ANY)
    bf16, f32 = jnp.bfloat16, jnp.float32
    blocks = pltpu.VMEM((8, B, B), bf16)
    padded = pltpu.VMEM((12, 10, 8, B), f32)
    return pl.pallas_call(
        block_kernel,
        out_shape=[
            jax.ShapeDtypeStruct((256, B), bf16),
            jax.ShapeDtypeStruct((256, B), bf16),
            jax.ShapeDtypeStruct((B, 2 * B), bf16),
            jax.ShapeDtypeStruct((2 * B, B), bf16),
            jax.ShapeDtypeStruct((2, 32, B), f32),
            jax.ShapeDtypeStruct((8, B), f32),
        ],
        in_specs=[vmem, vmem, vmem, anywhere, anywhere, anywhere],
        out_specs=[vmem, vmem, anywhere, anywhere, vmem, vmem],
        scratch_shapes=[blocks] * 7
        + [
            pltpu.VMEM((8, 8, B), f32),
            pltpu.VMEM((27, B), f32),
            padded,
            padded,
            pltpu.VMEM((B, B), f32),
            pltpu.VMEM((B, B), f32),
            pltpu.VMEM((B, B), bf16),
            pltpu.VMEM((B, B), bf16),
            pltpu.VMEM((B, 128), f32),
            pltpu.VMEM((2, 2, 2, CHUNK, B), bf16),
            pltpu.VMEM((2, 2, 2, CHUNK, B), bf16),
            pltpu.VMEM((256, B), f32),
            pltpu.VMEM((256, 128), f32),
            pltpu.VMEM((32, 8, B), f32),
            pltpu.VMEM((8, 32, B), bf16),
            pltpu.VMEM((8, 8, 256), f32),
            pltpu.VMEM((16, 8, B), f32),
        ]
        + RowScatter.scratch() * 2
        + WeightScatter.scratch() * 2
        + [pltpu.SemaphoreType.DMA((6,)), pltpu.SemaphoreType.DMA((144,)), pltpu.SemaphoreType.DMA((144,))],
        compiler_params=pltpu.CompilerParams(
            collective_id=0, has_side_effects=True, vmem_limit_bytes=62 << 20
        ),
        name="block",
    )(tok, gout, gain, up, down, taps)


def per_device(tokens, grad_out, gain, up_weight, down_weight, conv_taps):
    tok = tokens.reshape(256, B)
    gout = grad_out.reshape(256, B)
    gain_rows = jnp.broadcast_to(gain[None], (8, B))
    mixed, grad_tokens, grad_up, grad_down, conv, last = block(
        tok, gout, gain_rows, up_weight, down_weight, conv_taps
    )
    grad_conv = conv[:, :27].transpose(1, 0, 2).reshape(27, 2 * B)
    return (
        mixed.reshape(tokens.shape),
        grad_tokens.reshape(tokens.shape),
        grad_up,
        grad_down,
        grad_conv,
        last[0],
    )


def solution(mesh):
    rows = P("dp", "seq", None, None, "fsdp")
    return jax.shard_map(
        per_device,
        mesh=mesh,
        in_specs=(rows, rows, P("fsdp"), P("seq", "fsdp"), P("fsdp", "seq"), P(None, "fsdp")),
        out_specs=(rows, rows, P("seq", "fsdp"), P("fsdp", "seq"), P(None, "fsdp"), P("fsdp")),
        check_vma=False,
    )
```

time: 334 us -> 218 us (0.65)
  blocking collectives: 49.1 us -> 0 us
  matrix products: 23.3 us -> 0 us
  other arithmetic: 17.1 us -> 0 us
  between operations: 14.4 us -> 0.68 us
  Pallas kernels: 194 us -> 204 us
  waiting for transfers between devices: 8.9 us -> 0 us
  starting transfers between devices: 8.74 us -> 0 us
  local copies, waits for them, and re-layouts: 17.7 us -> 9.39 us
    psum x2 -> x0, blocking collectives: 49.1 us -> none  [the longest x1 36.7 us: per_device(): lax.psum((wide, jnp.sum(d_norm * hat, axis=0)), ('dp', 'seq'))]
    dot_general x6 -> x0, matrix products: 23.3 us -> none  [the longest x1 4.54 us: per_device(): jnp.einsum('brd,rh->bdh', normed, d_lifted, **f32).astype(jnp.bfloat16)]
    pallas_call x2 -> x1, Pallas kernels: 194 us -> 204 us  [block(): pl.pallas_call(block_kernel, out_shape=[jax.ShapeDtypeStruct((256, B), bf...]
    ppermute x4 -> x0, waiting for transfers between devices: 8.88 us -> none  [the longest x2 8.88 us: with_halo(): high = lax.ppermute(block[:, 0:1], 'seq', backward)]
    ppermute x4 -> x0, starting transfers between devices: 8.7 us -> none  [the longest x2 5.72 us: with_halo(): low = lax.ppermute(block[:, 3:4], 'seq', forward)]
    unnamed x38 -> x14, local copies, waits for them, and re-layouts: 12.8 us -> 6.39 us
    convert_element_type x3 -> x0, other arithmetic: 6.25 us -> none  [the longest x1 3.69 us: per_device(): conv_apply(d_padded, taps, True).astype(jnp.bfloat16).reshape(512, B)]
    reduce_sum x4 -> x0, other arithmetic: 5.1 us -> none  [the longest x2 2.83 us: conv_grad(): jnp.sum(d_float * window.astype(jnp.float32), axis=(0, 1, 2, 3))]
  transfers between devices with their start and end apart: 5 -> 0, of which waited for: 2 -> 0; matrix products, arithmetic and copies ran while one was open for 7% -> 0% of each run, Pallas kernels for 33% -> 0%
where the time goes in v2:
time: 218 us; the launch traced here: 214 us
  Pallas kernels  204 us (94%)
  local copies, waits for them, and re-layouts  9.39 us (4%)
    pallas_call x1, Pallas kernels, block(): pl.pallas_call(block_kernel, out_shape=[jax.ShapeDtypeStruct((256, B), bf...  204 us
    unnamed x14, local copies, waits for them, and re-layouts  6.39 us

profile of v2, /device:TPU:0, one launch (start us, length us, event | category | flops | bytes accessed | tf_op | source)
XLA Modules:
  0.0 213.7 jit_solution(3242232400974516903)
XLA Ops:
  0.6 0.0 copy-start.3
  0.6 0.7 copy-done.3
  1.3 0.6 broadcast_in_dim.2.gain
  1.9 203.7 %block.1 = (bf16[256,512]{1,0:T(8,128)(2,1)}, bf16[256,512]{1,0:T(8,128)(2,1)}, bf16[512,1024]{1,0:T(8,128)(2,1)}, bf16[1024,512]{1,0:T(8,128)(2,1)}, f32[2,32,512]{2,1,0:T(8,128)}, /*index=5*/f32[8,512]{1,0:T(8,128)}) custom-call(bf16[256,512]{1,0:T(8,128)(2,1)} %bitcast.13, bf16[256,512]{1,0:T(8,128)(2,1)} %bitcast.14, f32[8,512]{1,0:T(8,128)} %broadcast_in_dim.2.gain, ...), custom_call_target="tpu_custom_call" | custom-call | tf_op jit(solution)/shard_map/block/pallas_call | solution.py:670
  205.6 0.0 copy-start.1
  205.6 1.4 slice.7
  207.0 0.9 slice_bitcast_fusion
  207.9 0.1 copy.12
  208.0 0.7 copy.13
  208.7 0.0 copy-start.2
  208.7 1.7 copy.18
  210.4 0.0 copy-done.2
  210.4 0.7 copy.19
  211.1 0.0 copy-done.1
  211.1 0.0 copy-start
  211.1 1.0 copy.20
  212.1 0.6 copy-done
  212.7 1.0 copy.21
  (1 shorter events, 0.0 us)
Async XLA Ops:
  0.6 0.7 copy-start.3
  205.6 5.6 %copy-start.1 = (bf16[512,1024]{1,0:T(8,128)(2,1)S(1)}, bf16[512,1024]{1,0:T(8,128)(2,1)}, u32[]{:S(2)}) copy-start(bf16[512,1024]{1,0:T(8,128)(2,1)} %get-tuple-element.26) | copy-start | bytes 3145732
  208.7 1.7 copy-start.2
  211.1 1.6 copy-start

commit v3 on v2

v3 whole, which is shorter than its diff:
```python
import jax
import jax.numpy as jnp
from jax import lax
from jax.experimental import pallas as pl
from jax.experimental.pallas import tpu as pltpu
from jax.sharding import PartitionSpec as P

MESH = pl.DeviceIdType.MESH
gelu_scale = 0.7978845608028654
gelu_cubic = 0.044715
epsilon = 1e-06
B = 512


class Place:
    def __init__(self):
        self.zl = lax.axis_index("dp")
        self.f = lax.axis_index("fsdp")
        self.s = lax.axis_index("seq")
        self.x, self.c = lax.div(self.f, 2), lax.rem(self.f, 2)
        self.zh, self.y = lax.div(self.s, 4), lax.rem(self.s, 4)
        self.xs = [lax.rem(self.x + k, 4) for k in range(4)]
        self.ys = [lax.rem(self.y + k, 4) for k in range(4)]
        self.other_zl = {"dp": 1 - self.zl}
        self.other_core = {"fsdp": self.feat(0, 1)}
        self.x_up, self.x_down = {"fsdp": self.feat(1)}, {"fsdp": self.feat(3)}
        self.other_zh = {"seq": self.slab(0, 1)}
        self.y_up, self.y_down = {"seq": self.slab(1)}, {"seq": self.slab(3)}
        self.x_far, self.y_far = {"fsdp": self.feat(2)}, {"seq": self.slab(2)}
        self.diagonal = {"dp": 1 - self.zl, "seq": self.slab(0, 1)}
        self.rb = self.zl * 2 + self.zh
        self.z_peers = [
            (self.other_zl, (1 - self.zl) * 2 + self.zh),
            (self.other_zh, self.zl * 2 + 1 - self.zh),
            (self.diagonal, 3 - self.rb),
        ]
        self.x_peers = [self.x_up, self.x_far, self.x_down]
        self.y_peers = [self.y_up, self.y_far, self.y_down]

    def feat(self, k, flip=0):
        return self.xs[k] * 2 + (1 - self.c if flip else self.c)

    def slab(self, k, flip=0):
        return (1 - self.zh if flip else self.zh) * 4 + self.ys[k]

    def partners(self):
        return self.x_peers + self.y_peers + [where for where, _ in self.z_peers] + [self.other_core]


class Wires:
    def __init__(self, send, recv):
        self.send, self.recv, self.copies, self.left = send, recv, [], 0

    def start(self, src, dst, where):
        i = len(self.copies)
        copy = pltpu.make_async_remote_copy(
            src_ref=src, dst_ref=dst, send_sem=self.send.at[i], recv_sem=self.recv.at[i],
            device_id=where, device_id_type=MESH,
        )
        copy.start()
        self.copies.append(copy)
        return copy

    def flush(self, until=None):
        for copy in self.copies[self.left : until]:
            copy.wait_send()
        self.left = len(self.copies) if until is None else until


def meet(partners):
    barrier = pltpu.get_barrier_semaphore()
    for where in partners:
        pl.semaphore_signal(barrier, inc=1, device_id=where, device_id_type=MESH)
    pl.semaphore_wait(barrier, len(partners))


class WeightGather:
    def __init__(self, me, wires, own, for_other, buf):
        self.me, self.wires, self.own, self.for_other, self.buf = me, wires, own, for_other, buf
        self.half = buf.shape[1] // 2

    def start_z(self):
        self.z = self.wires.start(self.for_other, self.buf.at[self.me.s], self.me.other_zh)

    def start_y(self):
        self.up = self.wires.start(self.own, self.buf.at[self.me.s], self.me.y_up)
        self.down = self.wires.start(self.own, self.buf.at[self.me.s], self.me.y_down)

    def forward(self, flip):
        me, buf = self.me, self.buf
        below, above = me.slab(3, flip), me.slab(1, flip)
        self.up.wait_recv()
        part = buf.at[below, pl.ds(0, self.half)]
        first = self.wires.start(part, part, me.y_up)
        self.down.wait_recv()
        part = buf.at[above, pl.ds(self.half, self.half)]
        return first, self.wires.start(part, part, me.y_down)

    def forward_own(self):
        self.far = self.forward(0)

    def start_other(self):
        self.z.wait_recv()
        block = self.buf.at[self.me.slab(0, 1)]
        self.up = self.wires.start(block, block, self.me.y_up)
        self.down = self.wires.start(block, block, self.me.y_down)

    def forward_other(self):
        self.far_other = self.forward(1)

    def wait_far(self):
        for copy in self.far:
            copy.wait_recv()

    def wait_far_other(self):
        for copy in self.far_other:
            copy.wait_recv()


class TokenGather:
    def __init__(self, me, wires, own, buf, part, partners):
        self.me, self.wires, self.own, self.buf = me, wires, own, buf
        self.partners = [where for where, _ in partners]
        self.parts = [part] + [place for _, place in partners]
        self.ring, self.far, self.cores = {}, {}, []

    def rows(self, i, half=None):
        if half is None:
            return pl.ds(pl.multiple_of(self.parts[i] * 256, 256), 256)
        return pl.ds(pl.multiple_of(self.parts[i] * 256 + half * 128, 128), 128)

    def start_z(self):
        dst = self.buf.at[self.me.f, self.rows(0)]
        self.z = [self.wires.start(self.own, dst, where) for where in self.partners]

    def start(self, i):
        me = self.me
        dst = self.buf.at[me.f, self.rows(i)]
        src = dst if i else self.own
        if i:
            self.z[i - 1].wait_recv()
        self.ring[i] = [self.wires.start(src, dst, where) for where in (me.x_up, me.x_down)]
        self.cores.append(self.wires.start(src, dst, me.other_core))

    def to_core(self, k, i):
        block = self.buf.at[self.me.feat(k), self.rows(i)]
        self.cores.append(self.wires.start(block, block, self.me.other_core))

    def forward(self, i):
        me, buf = self.me, self.buf
        self.ring[i][0].wait_recv()
        part = buf.at[me.feat(3), self.rows(i, 0)]
        first = self.wires.start(part, part, me.x_up)
        self.ring[i][1].wait_recv()
        part = buf.at[me.feat(1), self.rows(i, 1)]
        self.far[i] = first, self.wires.start(part, part, me.x_down)
        self.to_core(3, i)
        self.to_core(1, i)

    def finish(self, i):
        for copy in self.far[i]:
            copy.wait_recv()
        self.to_core(2, i)

    def wait_cores(self):
        for copy in self.cores:
            copy.wait_recv()


CHUNK = 64
HID = 256


def chunk(r, base=0):
    return pl.ds(pl.multiple_of(base + r * CHUNK, CHUNK), CHUNK)


def loop(count, body):
    def step(i, carry):
        body(i)
        return carry

    lax.fori_loop(0, count, step, 0)


def add_into(dst, *parts):
    def body(r):
        rows = chunk(r)
        total = parts[0][rows, :].astype(jnp.float32)
        for part in parts[1:]:
            total = total + part[rows, :].astype(jnp.float32)
        dst[rows, :] = total.astype(dst.dtype)

    loop(dst.shape[0] // CHUNK, body)


class RowScatter:
    def __init__(self, me, wires, terms, part, partners, from_core, from_far, from_near, from_z):
        self.me, self.wires, self.terms = me, wires, terms
        self.part, self.partners = part, partners
        self.from_core, self.from_far, self.from_near = from_core, from_far, from_near
        self.from_z = from_z
        self.side = terms.shape[1] // 2

    def start_core(self):
        me = self.me
        self.core = {}
        for k in (2, 1, 3, 0):
            self.core[k] = self.wires.start(
                self.terms.at[me.feat(k, 1)], self.from_core.at[me.xs[k]], me.other_core
            )

    def held(self, k):
        return self.terms.at[self.me.feat(k)]

    def join(self, k):
        self.core[k].wait_recv()
        add_into(self.held(k), self.held(k), self.from_core.at[self.me.xs[k]])

    def start_far(self):
        me, side = self.me, self.side
        self.join(2)
        self.far = [
            self.wires.start(self.held(2).at[pl.ds(0, side)], self.from_far.at[0], me.x_up),
            self.wires.start(self.held(2).at[pl.ds(side, side)], self.from_far.at[1], me.x_down),
        ]
        self.join(1)
        self.join(3)
        self.near = [
            self.wires.start(self.held(1).at[pl.ds(side, side)], self.from_near.at[0, pl.ds(side, side)], me.x_up),
            self.wires.start(self.held(3).at[pl.ds(0, side)], self.from_near.at[1, pl.ds(0, side)], me.x_down),
        ]
        self.join(0)

    def start_near(self):
        me, side = self.me, self.side
        self.far[0].wait_recv()
        part = self.held(1).at[pl.ds(0, side)]
        add_into(part, part, self.from_far.at[0])
        self.near.append(self.wires.start(part, self.from_near.at[0, pl.ds(0, side)], me.x_up))
        self.far[1].wait_recv()
        part = self.held(3).at[pl.ds(side, side)]
        add_into(part, part, self.from_far.at[1])
        self.near.append(self.wires.start(part, self.from_near.at[1, pl.ds(side, side)], me.x_down))

    def sums(self, part):
        rows = pl.ds(pl.multiple_of(part * 256, 256), 256)
        return [self.held(0).at[rows], self.from_near.at[0, rows], self.from_near.at[1, rows]]

    def start_z(self):
        for copy in self.near:
            copy.wait_recv()
        self.z = []
        for i, (where, part) in enumerate(self.partners):
            sums = self.sums(part)
            add_into(sums[0], *sums)
            self.z.append(self.wires.start(sums[0], self.from_z.at[i], where))

    def wait(self):
        for copy in self.z:
            copy.wait_recv()
        self.all = self.sums(self.part) + [self.from_z.at[i] for i in range(len(self.z))]

    def result(self, rows):
        total = self.all[0][rows, :].astype(jnp.float32)
        for part in self.all[1:]:
            total = total + part[rows, :].astype(jnp.float32)
        return total

    @staticmethod
    def scratch(rows, partners):
        blocks = lambda *shape: pltpu.VMEM(shape, jnp.bfloat16)
        return [
            blocks(4, rows, B),
            blocks(2, rows // 2, B),
            blocks(2, rows, B),
            blocks(partners, 256, B),
        ]


class WeightScatter:
    def __init__(self, me, wires, terms, part, from_far, from_near):
        rows = pl.ds(part * 256, 256)
        self.me, self.wires, self.rows = me, wires, rows
        self.block = lambda j: terms.at[j, rows]
        self.from_far = [from_far.at[i, rows] for i in range(2)]
        self.from_near = lambda i: from_near.at[i, rows]

    def start_far(self):
        me, y = self.me, self.me.ys
        self.far = [
            self.wires.start(self.block(y[2]), self.from_far[0], me.y_up),
            self.wires.start(self.block(4 + y[2]), self.from_far[1], me.y_down),
        ]

    def start_direct(self):
        me, y = self.me, self.me.ys
        self.near = [
            self.wires.start(self.block(4 + y[1]), self.from_near(1), me.y_up),
            self.wires.start(self.block(y[3]), self.from_near(2), me.y_down),
        ]

    def start_near(self):
        me, y = self.me, self.me.ys
        self.far[0].wait_recv()
        block = self.block(y[1])
        add_into(block, block, self.from_far[0])
        self.near.append(self.wires.start(block, self.from_near(0), me.y_up))
        self.far[1].wait_recv()
        block = self.block(4 + y[3])
        add_into(block, block, self.from_far[1])
        self.near.append(self.wires.start(block, self.from_near(3), me.y_down))

    def parts(self, zh):
        return [self.block(zh * 4 + self.me.y), self.from_near(zh), self.from_near(2 + zh)]


    def start_z(self, from_z):
        for copy in self.near:
            copy.wait_recv()
        self.from_z = from_z.at[self.rows]
        other = self.block(self.me.slab(0, 1))
        add_into(other, *self.parts(1 - self.me.zh))
        self.z = self.wires.start(other, self.from_z, self.me.other_zh)

    def start_out(self, out, sem):
        self.z.wait_recv()
        block = self.block(self.me.s)
        add_into(block, *self.parts(self.me.zh), self.from_z)
        self.last = [self.wires.start(block, out, self.me.other_zl)]
        self.here = pltpu.make_async_copy(block, out, sem)
        self.here.start()


    def start_quarters(self, out, sem):
        me = self.me
        for copy in self.near:
            copy.wait_recv()
        mine, other = self.block(me.s), self.block(me.slab(0, 1))
        add_into(other, *self.parts(1 - me.zh))
        self.last = [self.wires.start(other, out, where) for where in (me.other_zh, me.diagonal)]
        add_into(mine, *self.parts(me.zh))
        self.last.append(self.wires.start(mine, out, me.other_zl))
        self.here = pltpu.make_async_copy(mine, out, sem)
        self.here.start()

    def wait_out(self):
        for copy in self.last:
            copy.wait_recv()
        self.here.wait()

    @staticmethod
    def scratch(rows):
        blocks = lambda *shape: pltpu.VMEM(shape, jnp.bfloat16)
        return [blocks(2, rows, B), blocks(4, rows, B)]


class Halo:
    def __init__(self, me, wires, planes, came, field):
        self.me, self.wires, self.planes, self.came, self.field = me, wires, planes, came, field

    def start(self):
        me = self.me
        self.copies = [
            self.wires.start(self.planes.at[1], self.came.at[0], me.y_up),
            self.wires.start(self.planes.at[0], self.came.at[1], me.y_down),
        ]

    def wait(self):
        for copy in self.copies:
            copy.wait_recv()
        low_inside = (self.me.y != 0).astype(jnp.float32)
        high_inside = (self.me.y != 3).astype(jnp.float32)
        for snap in range(2):
            low = [self.came[0, snap * 2 + zh].astype(jnp.float32) for zh in range(2)]
            high = [self.came[1, snap * 2 + zh].astype(jnp.float32) for zh in range(2)]
            edges = [
                (0, 0, low[0] * low_inside),
                (1, 0, low[1] * low_inside + low[0] * (1.0 - low_inside)),
                (0, 5, high[0] * high_inside + high[1] * (1.0 - high_inside)),
                (1, 5, high[1] * high_inside),
            ]
            for zh, place, plane in edges:
                self.field[(snap * 2 + zh) * 6 + place, 1:9] = plane.reshape(8, 8, HID)


def put_rows(part, rows_of, field, planes):
    for p in range(4):
        rounded = rows_of(p).astype(jnp.bfloat16)
        field[part * 6 + 1 + p, 1:9] = rounded.astype(jnp.float32).reshape(8, 8, HID)
        if p in (0, 3):
            planes[p // 3, part] = rounded


def shift(value, by):
    cells = lax.broadcasted_iota(jnp.int32, value.shape, 1)
    moved = pltpu.roll(value, by % 8, 1)
    return jnp.where(cells == (0 if by == 1 else 7), 0.0, moved)


def conv_planes(field, taps, flipped, count, which, finish):
    def body(i):
        part, p = which(i)
        for lane in range(0, HID, 128):
            lanes = pl.ds(lane, 128)
            by_c = [None] * 3
            for a in range(3):
                for b in range(3):
                    window = field[part * 6 + p + a, pl.ds(b, 8), :, lanes]
                    for c in range(3):
                        index = a * 9 + b * 3 + c
                        index = 26 - index if flipped else index
                        term = window * taps[pl.ds(index, 1), lanes].reshape(1, 1, 128)
                        by_c[c] = term if by_c[c] is None else by_c[c] + term
            total = by_c[1] + shift(by_c[0], 1) + shift(by_c[2], -1)
            finish(chunk(part * 4 + p), lanes, total.reshape(CHUNK, 128))

    loop(count, body)


def inner(i):
    return lax.div(i, 2), 1 + lax.rem(i, 2)


def outer(i):
    return lax.div(i, 2), 3 * lax.rem(i, 2)


def gelu_pair(preact):
    inner_value = gelu_scale * (preact + gelu_cubic * preact * preact * preact)
    tangent = jnp.tanh(inner_value)
    value = 0.5 * preact * (1.0 + tangent)
    slope = 0.5 * (1.0 + tangent) + 0.5 * preact * (1.0 - tangent * tangent) * gelu_scale * (
        1.0 + 3.0 * gelu_cubic * preact * preact
    )
    return (value, slope)


def dot(left, right, left_dim, right_dim):
    return lax.dot_general(
        left, right, (((left_dim,), (right_dim,)), ((), ())), preferred_element_type=jnp.float32
    )


def block_kernel(
    tok, gout, gain, up, down, taps_all,
    mixed_out, tokens_out, up_out, down_out, conv_out, gain_out,
    T, G, U, D, N, PB, gains, taps, field, d_field, total, slope, active, d_lifted, inverse,
    lift_here, lift_came, planes, came, d_norm, row_part, conv_sums, conv_terms, row_pair, row_terms,
    gain_z, gain_terms,
    b0, b1, b2, b3, n0, n1, n2, n3, w0, w1, v0, v1, v2,
    local, send, recv,
):
    me = Place()
    meet(me.partners())
    wires = Wires(send, recv)
    hidden = pl.ds(pl.multiple_of(me.zl * B, B), B)
    quarter = pl.ds(pl.multiple_of(me.rb * HID, HID), HID)
    other_quarter = pl.ds(pl.multiple_of((me.zl * 2 + 1 - me.zh) * HID, HID), HID)
    up_own, down_own = up.at[:, hidden], down.at[quarter, :]
    u = WeightGather(me, wires, up_own, up_own, U)
    d = WeightGather(me, wires, down_own, down.at[other_quarter, :], D)
    t = TokenGather(me, wires, tok, T, me.zl, [(me.other_zl, 1 - me.zl)])
    g = TokenGather(me, wires, gout, G, me.rb, me.z_peers)
    PN, GU, GD, d_slabs = N, G, T, lift_here
    b = RowScatter(me, wires, PB, me.rb, me.z_peers, b0, b1, b2, b3)
    n = RowScatter(me, wires, PN, me.zl, [(me.other_zl, 1 - me.zl)], n0, n1, n2, n3)
    gd = WeightScatter(me, wires, GD, 0, w0, w1)
    gus = [WeightScatter(me, wires, GU, part, v0, v1) for part in range(2)]

    t.start_z()
    u.start_z()
    u.start_y()
    t.start(0)
    gain_copies = [wires.start(gain, gains.at[me.f], where) for where in me.x_peers + [me.other_core]]
    here = [
        pltpu.make_async_copy(src, dst, local.at[i])
        for i, (src, dst) in enumerate(
            [
                (tok, T.at[me.f, t.rows(0)]),
                (gain, gains.at[me.f]),
                (up_own, U.at[me.s]),
                (taps_all.at[:, quarter], taps),
                (gout, G.at[me.f, g.rows(0)]),
                (down_own, D.at[me.s]),
            ]
        )
    ]
    for copy in here:
        copy.start()
    field[...] = jnp.zeros_like(field)
    d_field[...] = jnp.zeros_like(d_field)
    t.forward(0)
    t.start(1)
    g.start_z()
    for copy in gain_copies[:3]:
        copy.wait_recv()
    for k in (1, 2, 3):
        block = gains.at[me.feat(k)]
        gain_copies.append(wires.start(block, block, me.other_core))
    u.forward_own()
    u.start_other()
    d.start_z()
    t.finish(0)
    g.start(0)
    t.forward(1)
    d.start_y()
    t.finish(1)
    g.forward(0)
    g.start(1)
    for copy in here:
        copy.wait()
    for copy in gain_copies[3:]:
        copy.wait_recv()
    t.wait_cores()

    def normalise(r):
        rows = chunk(r)
        squares = jnp.zeros((CHUNK, 128), jnp.float32)
        for k in range(8):
            for lane in range(0, B, 128):
                value = T[k, rows, pl.ds(lane, 128)].astype(jnp.float32)
                squares = squares + value * value
        mean = jnp.sum(squares, axis=1, keepdims=True) / 4096.0
        inv = jnp.broadcast_to(lax.rsqrt(mean + epsilon), (CHUNK, 128))
        inverse[rows, :] = inv
        for k in range(8):
            for lane in range(0, B, 128):
                lanes = pl.ds(lane, 128)
                value = T[k, rows, lanes].astype(jnp.float32) * inv * gains[k, 0:1, lanes]
                N[k, rows, lanes] = value.astype(jnp.bfloat16)

    loop(8, normalise)
    total[...] = jnp.zeros_like(total)

    def lift(zh):
        def body(i):
            j = zh * 4 + i
            for half in range(2):
                total[pl.ds(half * B, B), :] += dot(N[j], U[j, :, pl.ds(half * HID, HID)], 1, 0)

        loop(4, body)

    u.wait_far()
    u.forward_other()
    lift(me.zh)
    g.finish(0)
    g.forward(1)
    g.start(2)
    d.forward_own()
    d.start_other()
    u.wait_far_other()
    lift(1 - me.zh)

    def round_lift(r):
        lift_here[chunk(r), :] = total[chunk(r), :].astype(jnp.bfloat16)

    loop(16, round_lift)
    lift_side = lambda zh: lift_here.at[pl.ds(pl.multiple_of(zh * B, B), B)]
    lift_copy = wires.start(lift_side(1 - me.zh), lift_came, me.other_zh)
    g.finish(1)
    g.forward(2)
    g.start(3)
    mine = lift_side(me.zh)
    for snap in range(2):
        put_rows(snap * 2 + me.zh, lambda p: mine[pl.ds(snap * 256 + p * CHUNK, CHUNK), :], field, planes.at[0])
    lift_copy.wait_recv()
    for snap in range(2):
        put_rows(
            snap * 2 + 1 - me.zh, lambda p: lift_came[pl.ds(snap * 256 + p * CHUNK, CHUNK), :], field, planes.at[0]
        )
    halo = Halo(me, wires, planes.at[0], came.at[0], field)
    halo.start()

    def activate(rows, lanes, preact):
        value, rate = gelu_pair(preact)
        active[rows, lanes] = value.astype(jnp.bfloat16)
        slope[rows, lanes] = rate

    conv_planes(field, taps, False, 8, inner, activate)
    d.wait_far()
    d.forward_other()
    halo.wait()
    conv_planes(field, taps, False, 8, outer, activate)
    g.finish(2)
    g.forward(3)
    d.wait_far_other()
    g.finish(3)
    g.wait_cores()
    gathered = len(wires.copies)
    total[...] = jnp.zeros_like(total)

    def d_active(j):
        total[...] += dot(G[j], D[j], 1, 1)

    loop(8, d_active)

    def d_preact(i):
        part = i
        put_rows(
            part,
            lambda p: total[chunk(part * 4 + p), :] * slope[chunk(part * 4 + p), :],
            d_field,
            planes.at[1],
        )

    loop(4, d_preact)
    d_halo = Halo(me, wires, planes.at[1], came.at[1], d_field)
    d_halo.start()

    wires.flush(gathered)

    def down_term(j):
        GD[j, pl.ds(0, HID), :] = dot(active[...], G[j], 0, 0).astype(jnp.bfloat16)

    loop(8, down_term)
    gd.start_far()
    gd.start_direct()

    def d_lift(rows, lanes, value):
        d_slabs[rows, lanes] = value.astype(jnp.bfloat16)

    conv_planes(d_field, taps, True, 8, inner, d_lift)
    d_halo.wait()
    conv_planes(d_field, taps, True, 8, outer, d_lift)
    d_columns = pl.ds(pl.multiple_of(me.zh * HID, HID), HID)
    d_copies = [
        wires.start(
            d_slabs.at[pl.ds(pl.multiple_of((snap * 2 + 1 - me.zh) * 256, 256), 256), :],
            d_lifted.at[pl.ds(snap * 256, 256), d_columns],
            me.other_zh,
        )
        for snap in range(2)
    ]
    for snap in range(2):
        d_lifted[pl.ds(snap * 256, 256), d_columns] = d_slabs[
            pl.ds(pl.multiple_of((snap * 2 + me.zh) * 256, 256), 256), :
        ]

    def branch_term(j):
        PB[j] = dot(active[...], D[j], 1, 0).astype(jnp.bfloat16)

    loop(8, branch_term)
    b.start_core()
    b.start_far()
    for copy in d_copies:
        copy.wait_recv()

    def up_term(j):
        GU[j, pl.ds(0, B), :] = dot(N[j], d_lifted[...], 0, 0).astype(jnp.bfloat16)

    loop(8, up_term)
    for part in gus:
        part.start_far()
    gd.start_near()

    def norm_term(j):
        PN[j] = dot(d_lifted[...], U[j], 1, 1).astype(jnp.bfloat16)

    loop(8, norm_term)
    n.start_core()
    for part in gus:
        part.start_direct()
    b.start_near()
    n.start_far()

    conv_sums[...] = jnp.zeros_like(conv_sums)

    def taps_grad(i):
        part, p = lax.div(i, 4), lax.rem(i, 4)
        for lane in range(0, HID, 128):
            lanes = pl.ds(lane, 128)
            here_d = d_field[part * 6 + 1 + p, pl.ds(1, 8), :, lanes]
            by_c = [shift(here_d, -1), here_d, shift(here_d, 1)]
            for a in range(3):
                for b_ in range(3):
                    window = field[part * 6 + p + a, pl.ds(b_, 8), :, lanes]
                    for c in range(3):
                        term = jnp.sum(by_c[c] * window, axis=0)
                        conv_sums[a * 9 + b_ * 3 + c, :, lanes] += term

    loop(16, taps_grad)
    conv_terms[me.y] = jnp.sum(conv_sums[...], axis=1).astype(jnp.bfloat16)
    conv_copies = [wires.start(conv_terms.at[me.y], conv_terms.at[me.y], where) for where in me.y_peers]

    gd.start_quarters(down_out.at[quarter, :], local.at[0])
    gus[0].start_near()
    gus[1].start_near()
    b.start_z()
    n.start_near()
    b.wait()

    def mix(r):
        rows = chunk(r)
        mixed_out[rows, :] = (tok[rows, :].astype(jnp.float32) + b.result(rows)).astype(jnp.bfloat16)

    loop(4, mix)
    for copy in conv_copies:
        copy.wait_recv()
    conv = conv_terms[0].astype(jnp.float32)
    for k in range(1, 4):
        conv = conv + conv_terms[k].astype(jnp.float32)
    conv_out[me.rb] = conv
    last_copies = [wires.start(conv_out.at[me.rb], conv_out.at[me.rb], where) for where, _ in me.z_peers]
    gus[0].start_z(v2)
    n.start_z()
    n.wait()

    def rows_part(r, gain_sum):
        rows = chunk(r)
        whole = n.result(rows)
        d_norm[rows, :] = whole
        inv = inverse[chunk(r, me.zl * 256), :]
        part = jnp.zeros((CHUNK, 128), jnp.float32)
        sums = []
        for lane in range(0, B, 128):
            lanes = slice(lane, lane + 128)
            with_hat = whole[:, lanes] * (tok[rows, lanes].astype(jnp.float32) * inv)
            part = part + with_hat * gain[0:1, lanes]
            sums.append(jnp.sum(with_hat.reshape(8, 8, 128), axis=0))
        row_part[rows, :] = part
        return gain_sum + jnp.concatenate(sums, axis=1)

    gain_sum = lax.fori_loop(0, 4, rows_part, jnp.zeros((8, B), jnp.float32))
    row_sum = jnp.sum(jnp.transpose(row_part[...]), axis=0, keepdims=True)
    row_pair[me.c] = jnp.broadcast_to(row_sum, (8, 256))
    row_copy = wires.start(row_pair.at[me.c], row_pair.at[me.c], me.other_core)
    gain_z[me.rb] = jnp.broadcast_to(jnp.sum(gain_sum, axis=0, keepdims=True), (8, B))
    gain_copies = [wires.start(gain_z.at[me.rb], gain_z.at[me.rb], where) for where, _ in me.z_peers]
    row_copy.wait_recv()
    row_terms[me.x] = row_pair[0] + row_pair[1]
    row_copies = [wires.start(row_terms.at[me.x], row_terms.at[me.x], where) for where in me.x_peers]
    gus[1].start_z(v2)
    for copy in gain_copies:
        copy.wait_recv()
    gain_terms[me.y] = (gain_z[0] + gain_z[1]) + (gain_z[2] + gain_z[3])
    last_copies += [wires.start(gain_terms.at[me.y], gain_terms.at[me.y], where) for where in me.y_peers]
    for copy in row_copies:
        copy.wait_recv()
    rows_sum = (row_terms[0] + row_terms[1]) + (row_terms[2] + row_terms[3])
    row_part[...] = jnp.transpose(jnp.broadcast_to(rows_sum[0:1, :], (128, 256)))
    gus[0].start_out(up_out.at[pl.ds(0, 256), hidden], local.at[1])

    def finish(r):
        rows = chunk(r)
        inv = inverse[chunk(r, me.zl * 256), :]
        share = row_part[rows, :] / 4096.0
        for lane in range(0, B, 128):
            lanes = slice(lane, lane + 128)
            hat = tok[rows, lanes].astype(jnp.float32) * inv
            value = inv * (d_norm[rows, lanes] * gain[0:1, lanes] - hat * share)
            tokens_out[rows, lanes] = (gout[rows, lanes].astype(jnp.float32) + value).astype(jnp.bfloat16)

    loop(4, finish)
    gus[1].start_out(up_out.at[pl.ds(256, 256), hidden], local.at[2])
    for copy in last_copies:
        copy.wait_recv()
    gain_out[...] = (gain_terms[0] + gain_terms[1]) + (gain_terms[2] + gain_terms[3])
    for part in [gd] + gus:
        part.wait_out()
    wires.flush()


def block(tok, gout, gain, up, down, taps):
    vmem = pl.BlockSpec(memory_space=pltpu.VMEM)
    anywhere = pl.BlockSpec(memory_space=pl.ANY)
    bf16, f32 = jnp.bfloat16, jnp.float32
    blocks = lambda *shape: pltpu.VMEM(shape, bf16)
    floats = lambda *shape: pltpu.VMEM(shape, f32)
    return pl.pallas_call(
        block_kernel,
        out_shape=[
            jax.ShapeDtypeStruct((256, B), bf16),
            jax.ShapeDtypeStruct((256, B), bf16),
            jax.ShapeDtypeStruct((B, 2 * B), bf16),
            jax.ShapeDtypeStruct((2 * B, B), bf16),
            jax.ShapeDtypeStruct((4, 32, HID), f32),
            jax.ShapeDtypeStruct((8, B), f32),
        ],
        in_specs=[vmem, vmem, vmem, anywhere, anywhere, anywhere],
        out_specs=[vmem, vmem, anywhere, anywhere, vmem, vmem],
        scratch_shapes=[
            blocks(8, B, B),
            blocks(8, 2 * B, B),
            blocks(8, B, B),
            blocks(8, HID, B),
            blocks(8, B, B),
            blocks(8, 2 * B, B),
            floats(8, 8, B),
            floats(27, HID),
            floats(24, 10, 8, HID),
            floats(24, 10, 8, HID),
            floats(2 * B, HID),
            floats(2 * B, HID),
            blocks(2 * B, HID),
            blocks(B, B),
            floats(B, 128),
            blocks(2 * B, HID),
            blocks(B, HID),
            blocks(2, 2, 4, CHUNK, HID),
            blocks(2, 2, 4, CHUNK, HID),
            floats(256, B),
            floats(256, 128),
            floats(32, 8, HID),
            blocks(4, 32, HID),
            floats(2, 8, 256),
            floats(4, 8, 256),
            floats(4, 8, B),
            floats(4, 8, B),
        ]
        + RowScatter.scratch(2 * B, 3)
        + RowScatter.scratch(B, 1)
        + WeightScatter.scratch(HID)
        + WeightScatter.scratch(B)
        + [blocks(B, B)]
        + [pltpu.SemaphoreType.DMA((6,)), pltpu.SemaphoreType.DMA((176,)), pltpu.SemaphoreType.DMA((176,))],
        compiler_params=pltpu.CompilerParams(
            collective_id=0, has_side_effects=True, vmem_limit_bytes=62 << 20
        ),
        name="block",
    )(tok, gout, gain, up, down, taps)


def per_device(tokens, grad_out, gain, up_weight, down_weight, conv_taps):
    tok = tokens.reshape(256, B)
    gout = grad_out.reshape(256, B)
    gain_rows = jnp.broadcast_to(gain[None], (8, B))
    mixed, grad_tokens, grad_up, grad_down, conv, last = block(
        tok, gout, gain_rows, up_weight, down_weight, conv_taps
    )
    grad_conv = conv[:, :27].transpose(1, 0, 2).reshape(27, 2 * B)
    return (
        mixed.reshape(tokens.shape),
        grad_tokens.reshape(tokens.shape),
        grad_up,
        grad_down,
        grad_conv,
        last[0],
    )


def solution(mesh):
    rows = P("dp", "seq", None, None, "fsdp")
    return jax.shard_map(
        per_device,
        mesh=mesh,
        in_specs=(rows, rows, P("fsdp"), P("seq", "fsdp"), P("fsdp", "seq"), P(None, "fsdp")),
        out_specs=(rows, rows, P("seq", "fsdp"), P("fsdp", "seq"), P(None, "fsdp"), P("fsdp")),
        check_vma=False,
    )
```

time: 218 us -> 189 us (0.87); the launches traced: 214 us -> 188 us
  Pallas kernels: 204 us -> 178 us
    pallas_call x1, Pallas kernels: 204 us -> 178 us  [block(): pl.pallas_call(block_kernel, out_shape=[jax.ShapeDtypeStruct((256, B), bf...]
where the time goes in v3:
time: 189 us; the launch traced here: 188 us
  Pallas kernels  178 us (94%)
  local copies, waits for them, and re-layouts  9.35 us (5%)
    pallas_call x1, Pallas kernels, block(): pl.pallas_call(block_kernel, out_shape=[jax.ShapeDtypeStruct((256, B), bf...  178 us
    unnamed x14, local copies, waits for them, and re-layouts  6.37 us

profile of v3, /device:TPU:0, one launch (start us, length us, event | category | flops | bytes accessed | tf_op | source)
XLA Modules:
  0.0 188.1 jit_solution(5490541697610011607)
XLA Ops:
  0.6 0.0 copy-start.3
  0.6 0.7 copy-done.3
  1.3 0.6 broadcast_in_dim.2.gain
  1.9 178.1 %block.1 = (bf16[256,512]{1,0:T(8,128)(2,1)}, bf16[256,512]{1,0:T(8,128)(2,1)}, bf16[512,1024]{1,0:T(8,128)(2,1)}, bf16[1024,512]{1,0:T(8,128)(2,1)}, f32[4,32,256]{2,1,0:T(8,128)}, /*index=5*/f32[8,512]{1,0:T(8,128)}) custom-call(bf16[256,512]{1,0:T(8,128)(2,1)} %bitcast.13, bf16[256,512]{1,0:T(8,128)(2,1)} %bitcast.14, f32[8,512]{1,0:T(8,128)} %broadcast_in_dim.2.gain, ...), custom_call_target="tpu_custom_call" | custom-call | tf_op jit(solution)/shard_map/block/pallas_call | solution.py:770
  180.0 0.0 copy-start.1
  180.0 1.4 slice.7
  181.4 0.9 slice_bitcast_fusion
  182.3 0.1 copy.12
  182.4 0.7 copy.13
  183.1 0.0 copy-start.2
  183.1 1.7 copy.18
  184.8 0.0 copy-done.2
  184.8 0.7 copy.19
  185.5 0.0 copy-done.1
  185.5 0.0 copy-start
  185.5 1.0 copy.20
  186.5 0.6 copy-done
  187.1 1.0 copy.21
  (1 shorter events, 0.0 us)
Async XLA Ops:
  0.6 0.7 copy-start.3
  180.0 5.5 %copy-start.1 = (bf16[512,1024]{1,0:T(8,128)(2,1)S(1)}, bf16[512,1024]{1,0:T(8,128)(2,1)}, u32[]{:S(2)}) copy-start(bf16[512,1024]{1,0:T(8,128)(2,1)} %get-tuple-element.26) | copy-start | bytes 3145732
  183.1 1.7 copy-start.2
  185.5 1.6 copy-start

commit v4 on v3

--- a/solution.py
+++ b/solution.py
@@ -279,8 +279,8 @@
 
 
 class WeightScatter:
-    def __init__(self, me, wires, terms, part, from_far, from_near):
-        rows = pl.ds(part * 256, 256)
+    def __init__(self, me, wires, terms, start, size, from_far, from_near):
+        rows = pl.ds(start, size)
         self.me, self.wires, self.rows = me, wires, rows
         self.block = lambda j: terms.at[j, rows]
         self.from_far = [from_far.at[i, rows] for i in range(2)]
@@ -465,11 +465,10 @@
     PN, GU, GD, d_slabs = N, G, T, lift_here
     b = RowScatter(me, wires, PB, me.rb, me.z_peers, b0, b1, b2, b3)
     n = RowScatter(me, wires, PN, me.zl, [(me.other_zl, 1 - me.zl)], n0, n1, n2, n3)
-    gd = WeightScatter(me, wires, GD, 0, w0, w1)
-    gus = [WeightScatter(me, wires, GU, part, v0, v1) for part in range(2)]
+    gd = WeightScatter(me, wires, GD, 0, HID, w0, w1)
+    gus = [WeightScatter(me, wires, GU, i * 128, 128, v0, v1) for i in range(4)]
 
     t.start_z()
-    u.start_z()
     u.start_y()
     t.start(0)
     gain_copies = [wires.start(gain, gains.at[me.f], where) for where in me.x_peers + [me.other_core]]
@@ -488,6 +487,8 @@
     ]
     for copy in here:
         copy.start()
+    u.start_z()
+    g.start(0)
     field[...] = jnp.zeros_like(field)
     d_field[...] = jnp.zeros_like(d_field)
     t.forward(0)
@@ -499,15 +500,15 @@
         block = gains.at[me.feat(k)]
         gain_copies.append(wires.start(block, block, me.other_core))
     u.forward_own()
+    t.finish(0)
+    g.forward(0)
+    t.forward(1)
     u.start_other()
     d.start_z()
-    t.finish(0)
-    g.start(0)
-    t.forward(1)
+    g.start(1)
+    t.finish(1)
     d.start_y()
-    t.finish(1)
-    g.forward(0)
-    g.start(1)
+    g.start(2)
     for copy in here:
         copy.wait()
     for copy in gain_copies[3:]:
@@ -543,10 +544,10 @@
 
     u.wait_far()
     u.forward_other()
-    lift(me.zh)
     g.finish(0)
     g.forward(1)
-    g.start(2)
+    g.start(3)
+    lift(me.zh)
     d.forward_own()
     d.start_other()
     u.wait_far_other()
@@ -560,7 +561,6 @@
     lift_copy = wires.start(lift_side(1 - me.zh), lift_came, me.other_zh)
     g.finish(1)
     g.forward(2)
-    g.start(3)
     mine = lift_side(me.zh)
     for snap in range(2):
         put_rows(snap * 2 + me.zh, lambda p: mine[pl.ds(snap * 256 + p * CHUNK, CHUNK), :], field, planes.at[0])
@@ -585,6 +585,12 @@
     g.finish(2)
     g.forward(3)
     d.wait_far_other()
+
+    def branch_term(j):
+        PB[j] = dot(active[...], D[j], 1, 0).astype(jnp.bfloat16)
+
+    loop(8, branch_term)
+    b.start_core()
     g.finish(3)
     g.wait_cores()
     gathered = len(wires.copies)
@@ -608,6 +614,7 @@
     d_halo = Halo(me, wires, planes.at[1], came.at[1], d_field)
     d_halo.start()
 
+    b.start_far()
     wires.flush(gathered)
 
     def down_term(j):
@@ -636,15 +643,10 @@
         d_lifted[pl.ds(snap * 256, 256), d_columns] = d_slabs[
             pl.ds(pl.multiple_of((snap * 2 + me.zh) * 256, 256), 256), :
         ]
-
-    def branch_term(j):
-        PB[j] = dot(active[...], D[j], 1, 0).astype(jnp.bfloat16)
-
-    loop(8, branch_term)
-    b.start_core()
-    b.start_far()
     for copy in d_copies:
         copy.wait_recv()
+    b.start_near()
+    gd.start_near()
 
     def up_term(j):
         GU[j, pl.ds(0, B), :] = dot(N[j], d_lifted[...], 0, 0).astype(jnp.bfloat16)
@@ -652,16 +654,12 @@
     loop(8, up_term)
     for part in gus:
         part.start_far()
-    gd.start_near()
 
     def norm_term(j):
         PN[j] = dot(d_lifted[...], U[j], 1, 1).astype(jnp.bfloat16)
 
     loop(8, norm_term)
     n.start_core()
-    for part in gus:
-        part.start_direct()
-    b.start_near()
     n.start_far()
 
     conv_sums[...] = jnp.zeros_like(conv_sums)
@@ -684,26 +682,28 @@
     conv_copies = [wires.start(conv_terms.at[me.y], conv_terms.at[me.y], where) for where in me.y_peers]
 
     gd.start_quarters(down_out.at[quarter, :], local.at[0])
-    gus[0].start_near()
-    gus[1].start_near()
-    b.start_z()
+    for part in gus[:2]:
+        part.start_direct()
+        part.start_near()
     n.start_near()
-    b.wait()
-
-    def mix(r):
-        rows = chunk(r)
-        mixed_out[rows, :] = (tok[rows, :].astype(jnp.float32) + b.result(rows)).astype(jnp.bfloat16)
-
-    loop(4, mix)
     for copy in conv_copies:
         copy.wait_recv()
     conv = conv_terms[0].astype(jnp.float32)
     for k in range(1, 4):
         conv = conv + conv_terms[k].astype(jnp.float32)
-    conv_out[me.rb] = conv
-    last_copies = [wires.start(conv_out.at[me.rb], conv_out.at[me.rb], where) for where, _ in me.z_peers]
+    conv_here = conv_out.at[:, quarter]
+    conv_here[...] = conv
+    last_copies = [wires.start(conv_here, conv_here, where) for where, _ in me.z_peers]
     gus[0].start_z(v2)
+    gus[2].start_direct()
+    gus[2].start_near()
+    b.start_z()
+    gus[1].start_z(v2)
+    gus[3].start_direct()
+    gus[3].start_near()
     n.start_z()
+    up_rows = lambda i: up_out.at[pl.ds(i * 128, 128), hidden]
+    gus[0].start_out(up_rows(0), local.at[1])
     n.wait()
 
     def rows_part(r, gain_sum):
@@ -730,7 +730,8 @@
     row_copy.wait_recv()
     row_terms[me.x] = row_pair[0] + row_pair[1]
     row_copies = [wires.start(row_terms.at[me.x], row_terms.at[me.x], where) for where in me.x_peers]
-    gus[1].start_z(v2)
+    gus[2].start_z(v2)
+    gus[1].start_out(up_rows(1), local.at[2])
     for copy in gain_copies:
         copy.wait_recv()
     gain_terms[me.y] = (gain_z[0] + gain_z[1]) + (gain_z[2] + gain_z[3])
@@ -739,7 +740,8 @@
         copy.wait_recv()
     rows_sum = (row_terms[0] + row_terms[1]) + (row_terms[2] + row_terms[3])
     row_part[...] = jnp.transpose(jnp.broadcast_to(rows_sum[0:1, :], (128, 256)))
-    gus[0].start_out(up_out.at[pl.ds(0, 256), hidden], local.at[1])
+    gus[3].start_z(v2)
+    gus[2].start_out(up_rows(2), local.at[3])
 
     def finish(r):
         rows = chunk(r)
@@ -752,10 +754,17 @@
             tokens_out[rows, lanes] = (gout[rows, lanes].astype(jnp.float32) + value).astype(jnp.bfloat16)
 
     loop(4, finish)
-    gus[1].start_out(up_out.at[pl.ds(256, 256), hidden], local.at[2])
+    gus[3].start_out(up_rows(3), local.at[4])
+    b.wait()
+
+    def mix(r):
+        rows = chunk(r)
+        mixed_out[rows, :] = (tok[rows, :].astype(jnp.float32) + b.result(rows)).astype(jnp.bfloat16)
+
+    loop(4, mix)
     for copy in last_copies:
         copy.wait_recv()
-    gain_out[...] = (gain_terms[0] + gain_terms[1]) + (gain_terms[2] + gain_terms[3])
+    gain_out[...] = ((gain_terms[0] + gain_terms[1]) + (gain_terms[2] + gain_terms[3]))[0:1, :]
     for part in [gd] + gus:
         part.wait_out()
     wires.flush()
@@ -774,8 +783,8 @@
             jax.ShapeDtypeStruct((256, B), bf16),
             jax.ShapeDtypeStruct((B, 2 * B), bf16),
             jax.ShapeDtypeStruct((2 * B, B), bf16),
-            jax.ShapeDtypeStruct((4, 32, HID), f32),
-            jax.ShapeDtypeStruct((8, B), f32),
+            jax.ShapeDtypeStruct((32, 2 * B), f32),
+            jax.ShapeDtypeStruct((1, B), f32),
         ],
         in_specs=[vmem, vmem, vmem, anywhere, anywhere, anywhere],
         out_specs=[vmem, vmem, anywhere, anywhere, vmem, vmem],
@@ -813,7 +822,7 @@
         + WeightScatter.scratch(HID)
         + WeightScatter.scratch(B)
         + [blocks(B, B)]
-        + [pltpu.SemaphoreType.DMA((6,)), pltpu.SemaphoreType.DMA((176,)), pltpu.SemaphoreType.DMA((176,))],
+        + [pltpu.SemaphoreType.DMA((6,)), pltpu.SemaphoreType.DMA((200,)), pltpu.SemaphoreType.DMA((200,))],
         compiler_params=pltpu.CompilerParams(
             collective_id=0, has_side_effects=True, vmem_limit_bytes=62 << 20
         ),
@@ -821,21 +830,52 @@
     )(tok, gout, gain, up, down, taps)
 
 
+def place_kernel(*refs):
+    count = len(refs) // 3
+    ins, outs, held, cut, sems = refs[:count], refs[count : 2 * count], refs[2 * count : -2], refs[-2], refs[-1]
+    arriving = [pltpu.make_async_copy(src, mid, sems.at[0, i]) for i, (src, mid) in enumerate(zip(ins, held))]
+    for copy in arriving:
+        copy.start()
+    leaving = []
+    for i, (mid, dst) in enumerate(zip(held, outs)):
+        arriving[i].wait()
+        src = mid
+        if mid.shape != dst.shape:
+            cut[...] = mid[: dst.shape[0], :]
+            src = cut
+        leaving.append(pltpu.make_async_copy(src, dst, sems.at[1, i]))
+        leaving[-1].start()
+    for copy in leaving:
+        copy.wait()
+
+
+def place(arrays, rows):
+    shapes = [(rows,) + a.shape[1:] if i == 4 else a.shape for i, a in enumerate(arrays)]
+    specs = [pl.BlockSpec(memory_space=pl.ANY)] * len(arrays)
+    return pl.pallas_call(
+        place_kernel,
+        out_shape=[jax.ShapeDtypeStruct(shape, a.dtype) for shape, a in zip(shapes, arrays)],
+        in_specs=specs,
+        out_specs=specs,
+        scratch_shapes=[pltpu.VMEM(a.shape, a.dtype) for a in arrays]
+        + [pltpu.VMEM(shapes[4], jnp.float32), pltpu.SemaphoreType.DMA((2, len(arrays)))],
+        name="place",
+    )(*arrays)
+
+
 def per_device(tokens, grad_out, gain, up_weight, down_weight, conv_taps):
     tok = tokens.reshape(256, B)
     gout = grad_out.reshape(256, B)
     gain_rows = jnp.broadcast_to(gain[None], (8, B))
-    mixed, grad_tokens, grad_up, grad_down, conv, last = block(
-        tok, gout, gain_rows, up_weight, down_weight, conv_taps
-    )
-    grad_conv = conv[:, :27].transpose(1, 0, 2).reshape(27, 2 * B)
+    outs = block(tok, gout, gain_rows, up_weight, down_weight, conv_taps)
+    mixed, grad_tokens, grad_up, grad_down, grad_conv, grad_gain = place(outs, conv_taps.shape[0])
     return (
         mixed.reshape(tokens.shape),
         grad_tokens.reshape(tokens.shape),
         grad_up,
         grad_down,
         grad_conv,
-        last[0],
+        grad_gain.reshape(B),
     )
 
 

time: 189 us -> 177 us (0.937)
  local copies, waits for them, and re-layouts: 9.35 us -> 1.28 us
  Pallas kernels: 178 us -> 175 us
    unnamed x14 -> x2, local copies, waits for them, and re-layouts: 6.37 us -> 0.67 us
    pallas_call x1, Pallas kernels: 178 us -> 172 us  [block(): pl.pallas_call(block_kernel, out_shape=[jax.ShapeDtypeStruct((256, B), bf...]
    pallas_call x0 -> x1, Pallas kernels: none -> 2.85 us  [place(): pl.pallas_call(place_kernel, out_shape=[jax.ShapeDtypeStruct(shape, a.dty...]
where the time goes in v4:
time: 177 us
  Pallas kernels  175 us (99%)
    pallas_call x1, Pallas kernels, block(): pl.pallas_call(block_kernel, out_shape=[jax.ShapeDtypeStruct((256, B), bf...  172 us

profile of v4, /device:TPU:0, one launch (start us, length us, event | category | flops | bytes accessed | tf_op | source)
XLA Modules:
  0.0 177.2 jit_solution(4244258302002743498)
XLA Ops:
  0.6 0.0 copy-start
  0.6 0.7 copy-done
  1.3 0.6 broadcast_in_dim.2.gain
  1.9 172.4 %block.1 = (bf16[256,512]{1,0:T(8,128)(2,1)}, bf16[256,512]{1,0:T(8,128)(2,1)}, bf16[512,1024]{1,0:T(8,128)(2,1)}, bf16[1024,512]{1,0:T(8,128)(2,1)}, f32[32,1024]{1,0:T(8,128)}, /*index=5*/f32[1,512]{1,0:T(1,128)}) custom-call(bf16[256,512]{1,0:T(8,128)(2,1)} %bitcast.5, bf16[256,512]{1,0:T(8,128)(2,1)} %bitcast.6, f32[8,512]{1,0:T(8,128)} %broadcast_in_dim.2.gain, ...), custom_call_target="tpu_custom_call" | custom-call | tf_op jit(solution)/shard_map/block/pallas_call | solution.py:779
  174.3 2.8 %place.1 = (bf16[256,512]{1,0:T(8,128)(2,1)}, bf16[256,512]{1,0:T(8,128)(2,1)}, bf16[512,1024]{1,0:T(8,128)(2,1)}, bf16[1024,512]{1,0:T(8,128)(2,1)}, f32[27,1024]{1,0:T(8,128)}, /*index=5*/f32[1,512]{1,0:T(1,128)}) custom-call(bf16[256,512]{1,0:T(8,128)(2,1)} %get-tuple-element.18.refs_0_, bf16[256,512]{1,0:T(8,128)(2,1)} %get-tuple-element.19.refs_1_, ...), custom_call_target="tpu_custom_call" | custom-call | tf_op jit(solution)/shard_map/place/pallas_call | solution.py:855
Async XLA Ops:
  0.6 0.7 copy-start

commit v5 on v4

--- a/solution.py
+++ b/solution.py
@@ -543,13 +543,15 @@
         loop(4, body)
 
     u.wait_far()
-    u.forward_other()
     g.finish(0)
     g.forward(1)
+    lift(me.zh)
+    u.forward_other()
+    d.forward_own()
     g.start(3)
-    lift(me.zh)
-    d.forward_own()
     d.start_other()
+    g.finish(1)
+    g.forward(2)
     u.wait_far_other()
     lift(1 - me.zh)
 
@@ -559,8 +561,10 @@
     loop(16, round_lift)
     lift_side = lambda zh: lift_here.at[pl.ds(pl.multiple_of(zh * B, B), B)]
     lift_copy = wires.start(lift_side(1 - me.zh), lift_came, me.other_zh)
-    g.finish(1)
-    g.forward(2)
+    g.forward(3)
+    d.wait_far()
+    d.forward_other()
+    g.finish(2)
     mine = lift_side(me.zh)
     for snap in range(2):
         put_rows(snap * 2 + me.zh, lambda p: mine[pl.ds(snap * 256 + p * CHUNK, CHUNK), :], field, planes.at[0])
@@ -578,12 +582,8 @@
         slope[rows, lanes] = rate
 
     conv_planes(field, taps, False, 8, inner, activate)
-    d.wait_far()
-    d.forward_other()
     halo.wait()
     conv_planes(field, taps, False, 8, outer, activate)
-    g.finish(2)
-    g.forward(3)
     d.wait_far_other()
 
     def branch_term(j):
@@ -639,6 +639,7 @@
         )
         for snap in range(2)
     ]
+    gd.start_near()
     for snap in range(2):
         d_lifted[pl.ds(snap * 256, 256), d_columns] = d_slabs[
             pl.ds(pl.multiple_of((snap * 2 + me.zh) * 256, 256), 256), :
@@ -646,7 +647,6 @@
     for copy in d_copies:
         copy.wait_recv()
     b.start_near()
-    gd.start_near()
 
     def up_term(j):
         GU[j, pl.ds(0, B), :] = dot(N[j], d_lifted[...], 0, 0).astype(jnp.bfloat16)
@@ -654,6 +654,7 @@
     loop(8, up_term)
     for part in gus:
         part.start_far()
+    gd.start_quarters(down_out.at[quarter, :], local.at[0])
 
     def norm_term(j):
         PN[j] = dot(d_lifted[...], U[j], 1, 1).astype(jnp.bfloat16)
@@ -681,7 +682,7 @@
     conv_terms[me.y] = jnp.sum(conv_sums[...], axis=1).astype(jnp.bfloat16)
     conv_copies = [wires.start(conv_terms.at[me.y], conv_terms.at[me.y], where) for where in me.y_peers]
 
-    gd.start_quarters(down_out.at[quarter, :], local.at[0])
+    b.start_z()
     for part in gus[:2]:
         part.start_direct()
         part.start_near()
@@ -697,13 +698,13 @@
     gus[0].start_z(v2)
     gus[2].start_direct()
     gus[2].start_near()
-    b.start_z()
+    n.start_z()
     gus[1].start_z(v2)
     gus[3].start_direct()
     gus[3].start_near()
-    n.start_z()
     up_rows = lambda i: up_out.at[pl.ds(i * 128, 128), hidden]
     gus[0].start_out(up_rows(0), local.at[1])
+    gus[2].start_z(v2)
     n.wait()
 
     def rows_part(r, gain_sum):
@@ -730,8 +731,9 @@
     row_copy.wait_recv()
     row_terms[me.x] = row_pair[0] + row_pair[1]
     row_copies = [wires.start(row_terms.at[me.x], row_terms.at[me.x], where) for where in me.x_peers]
-    gus[2].start_z(v2)
+    gus[3].start_z(v2)
     gus[1].start_out(up_rows(1), local.at[2])
+    gus[2].start_out(up_rows(2), local.at[3])
     for copy in gain_copies:
         copy.wait_recv()
     gain_terms[me.y] = (gain_z[0] + gain_z[1]) + (gain_z[2] + gain_z[3])
@@ -740,8 +742,7 @@
         copy.wait_recv()
     rows_sum = (row_terms[0] + row_terms[1]) + (row_terms[2] + row_terms[3])
     row_part[...] = jnp.transpose(jnp.broadcast_to(rows_sum[0:1, :], (128, 256)))
-    gus[3].start_z(v2)
-    gus[2].start_out(up_rows(2), local.at[3])
+    gus[3].start_out(up_rows(3), local.at[4])
 
     def finish(r):
         rows = chunk(r)
@@ -754,7 +755,6 @@
             tokens_out[rows, lanes] = (gout[rows, lanes].astype(jnp.float32) + value).astype(jnp.bfloat16)
 
     loop(4, finish)
-    gus[3].start_out(up_rows(3), local.at[4])
     b.wait()
 
     def mix(r):

time: 177 us -> 171 us (0.966)
  Pallas kernels: 175 us -> 169 us
    pallas_call x1, Pallas kernels: 172 us -> 166 us  [block(): pl.pallas_call(block_kernel, out_shape=[jax.ShapeDtypeStruct((256, B), bf...]
where the time goes in v5:
time: 171 us; the launch traced here: 170 us
  Pallas kernels  169 us (99%)
    pallas_call x1, Pallas kernels, block(): pl.pallas_call(block_kernel, out_shape=[jax.ShapeDtypeStruct((256, B), bf...  166 us

profile of v5, /device:TPU:0, one launch (start us, length us, event | category | flops | bytes accessed | tf_op | source)
XLA Modules:
  0.0 170.5 jit_solution(9064780592874683389)
XLA Ops:
  0.6 0.0 copy-start
  0.6 0.7 copy-done
  1.3 0.6 broadcast_in_dim.2.gain
  1.9 165.7 %block.1 = (bf16[256,512]{1,0:T(8,128)(2,1)}, bf16[256,512]{1,0:T(8,128)(2,1)}, bf16[512,1024]{1,0:T(8,128)(2,1)}, bf16[1024,512]{1,0:T(8,128)(2,1)}, f32[32,1024]{1,0:T(8,128)}, /*index=5*/f32[1,512]{1,0:T(1,128)}) custom-call(bf16[256,512]{1,0:T(8,128)(2,1)} %bitcast.5, bf16[256,512]{1,0:T(8,128)(2,1)} %bitcast.6, f32[8,512]{1,0:T(8,128)} %broadcast_in_dim.2.gain, ...), custom_call_target="tpu_custom_call" | custom-call | tf_op jit(solution)/shard_map/block/pallas_call | solution.py:779
  167.6 2.8 %place.1 = (bf16[256,512]{1,0:T(8,128)(2,1)}, bf16[256,512]{1,0:T(8,128)(2,1)}, bf16[512,1024]{1,0:T(8,128)(2,1)}, bf16[1024,512]{1,0:T(8,128)(2,1)}, f32[27,1024]{1,0:T(8,128)}, /*index=5*/f32[1,512]{1,0:T(1,128)}) custom-call(bf16[256,512]{1,0:T(8,128)(2,1)} %get-tuple-element.18.refs_0_, bf16[256,512]{1,0:T(8,128)(2,1)} %get-tuple-element.19.refs_1_, ...), custom_call_target="tpu_custom_call" | custom-call | tf_op jit(solution)/shard_map/place/pallas_call | solution.py:855
Async XLA Ops:
  0.6 0.7 copy-start

commit v6 on v5

--- a/solution.py
+++ b/solution.py
@@ -795,7 +795,7 @@
             blocks(8, HID, B),
             blocks(8, B, B),
             blocks(8, 2 * B, B),
-            floats(8, 8, B),
+            floats(8, 1, B),
             floats(27, HID),
             floats(24, 10, 8, HID),
             floats(24, 10, 8, HID),
@@ -866,8 +866,7 @@
 def per_device(tokens, grad_out, gain, up_weight, down_weight, conv_taps):
     tok = tokens.reshape(256, B)
     gout = grad_out.reshape(256, B)
-    gain_rows = jnp.broadcast_to(gain[None], (8, B))
-    outs = block(tok, gout, gain_rows, up_weight, down_weight, conv_taps)
+    outs = block(tok, gout, gain.reshape(1, B), up_weight, down_weight, conv_taps)
     mixed, grad_tokens, grad_up, grad_down, grad_conv, grad_gain = place(outs, conv_taps.shape[0])
     return (
         mixed.reshape(tokens.shape),

time: 171 us -> 169 us (0.988)
  no operation moved by 1% of the time
where the time goes in v6:
time: 169 us
  Pallas kernels  168 us (99%)
    pallas_call x1, Pallas kernels, block(): pl.pallas_call(block_kernel, out_shape=[jax.ShapeDtypeStruct((256, B), bf...  165 us

profile of v6, /device:TPU:0, one launch (start us, length us, event | category | flops | bytes accessed | tf_op | source)
XLA Modules:
  0.0 168.7 jit_solution(328127640143651035)
XLA Ops:
  0.6 165.2 %block.1 = (bf16[256,512]{1,0:T(8,128)(2,1)}, bf16[256,512]{1,0:T(8,128)(2,1)}, bf16[512,1024]{1,0:T(8,128)(2,1)}, bf16[1024,512]{1,0:T(8,128)(2,1)}, f32[32,1024]{1,0:T(8,128)}, /*index=5*/f32[1,512]{1,0:T(1,128)}) custom-call(bf16[256,512]{1,0:T(8,128)(2,1)} %bitcast.6, bf16[256,512]{1,0:T(8,128)(2,1)} %bitcast.7, f32[1,512]{1,0:T(1,128)} %bitcast.8, ...), custom_call_target="tpu_custom_call" | custom-call | tf_op jit(solution)/shard_map/block/pallas_call | solution.py:779
  165.8 2.8 %place.1 = (bf16[256,512]{1,0:T(8,128)(2,1)}, bf16[256,512]{1,0:T(8,128)(2,1)}, bf16[512,1024]{1,0:T(8,128)(2,1)}, bf16[1024,512]{1,0:T(8,128)(2,1)}, f32[27,1024]{1,0:T(8,128)}, /*index=5*/f32[1,512]{1,0:T(1,128)}) custom-call(bf16[256,512]{1,0:T(8,128)(2,1)} %get-tuple-element.18.refs_0_, bf16[256,512]{1,0:T(8,128)(2,1)} %get-tuple-element.19.refs_1_, ...), custom_call_target="tpu_custom_call" | custom-call | tf_op jit(solution)/shard_map/place/pallas_call | solution.py:855
